TPU v7x, 512 devices: a whole 4x8x8 slice. The times are simulated.
512 devices in a mesh: seq: 64 (over y, z), chan: 8 (over x, core).
Axes of the slice: x: 4, y: 8, z: 8, core: 2. Of those that a mesh axis runs over, the one named last changes fastest.
Arguments:
- signal: bfloat16 [8192, 4096], P('seq', 'chan'), may hold values from -6 to 6
- gates: bfloat16 [8192, 4096], P('seq', 'chan'), may hold values from -6 to 6
- filters: bfloat16 [8192, 4096], P('seq', 'chan'), may hold values from -1 to 1
- skip_gain: float32 [4096], P('chan'), may hold values from 0.5 to 1.5
- out_proj: bfloat16 [4096, 4096], P('chan', 'seq'), may hold values from -0.09375 to 0.09375
- cotangent: bfloat16 [8192, 4096], P('seq', 'chan'), may hold values from -6 to 6
Outputs:
- mixed: bfloat16 [8192, 4096], P('seq', 'chan')
- grad_signal: bfloat16 [8192, 4096], P('seq', 'chan')
- grad_gates: bfloat16 [8192, 4096], P('seq', 'chan')
- grad_filters: bfloat16 [8192, 4096], P('seq', 'chan')
All inputs are finite; a program needn't handle non-finite values.
Results may differ from a plain program's by a relative error of at most 0.01.
Values may be sent and summed in bfloat16 or wider, within the bound.
A program may use at most 64 MiB of HBM per device.

v0:
```python
import math

import jax
import jax.numpy as jnp
from jax import lax
from jax.sharding import PartitionSpec as P


def angles(numer, modulus):
    return 2.0 * math.pi / modulus * (numer % modulus).astype(jnp.float32)


def contract(spec, table, data):
    return jnp.einsum(spec, table, data, precision=lax.Precision.HIGHEST)


def row_tables(tok_dev):
    index_t = jnp.arange(tok_dev, dtype=jnp.int32)
    phase = angles(index_t[:, None] * index_t[None, :], tok_dev)
    return (jnp.cos(phase), jnp.sin(phase))


def forward_transform(drawn_numbers):
    tok_dev = drawn_numbers.shape[0]
    groups = lax.axis_size("seq")
    rows_per = tok_dev // groups
    modulus = 2 * tok_dev * groups
    position = lax.axis_index("seq")
    index_j = jnp.arange(groups, dtype=jnp.int32)
    index_k = jnp.arange(2 * groups, dtype=jnp.int32)
    first_phase = angles(index_k[:, None] * index_j[None, :], 2 * groups)
    first_cos = jnp.cos(first_phase)
    leading_sine_factor = jnp.sin(first_phase)
    local_rows = position * rows_per + jnp.arange(rows_per, dtype=jnp.int32)
    twist_angle = angles(index_k[:, None] * local_rows[None, :], modulus)
    twist_cos = jnp.cos(twist_angle)[:, :, None]
    twist_sin = jnp.sin(twist_angle)[:, :, None]
    blocks = drawn_numbers.reshape(groups, rows_per, drawn_numbers.shape[1])
    widened = lax.all_to_all(blocks, "seq", split_axis=0, concat_axis=0, tiled=True).astype(
        jnp.float32
    )
    real_a = contract("kj,jrc->krc", first_cos, widened)
    imag_a = -contract("kj,jrc->krc", leading_sine_factor, widened)
    mid_real = real_a * twist_cos + imag_a * twist_sin
    mid_imag = imag_a * twist_cos - real_a * twist_sin
    last_cos, last_sin = row_tables(tok_dev)
    real_p = lax.all_to_all(mid_real, "seq", split_axis=0, concat_axis=1, tiled=True)
    imag_p = lax.all_to_all(mid_imag, "seq", split_axis=0, concat_axis=1, tiled=True)
    spec_real = contract("qr,krc->kqc", last_cos, real_p) + contract(
        "qr,krc->kqc", last_sin, imag_p
    )
    spec_imag = contract("qr,krc->kqc", last_cos, imag_p) - contract(
        "qr,krc->kqc", last_sin, real_p
    )
    return (spec_real, spec_imag)


def inverse_transform(spec_real, spec_imag, keep_imag):
    tok_dev = spec_real.shape[1]
    groups = lax.axis_size("seq")
    modulus = 2 * tok_dev * groups
    position = lax.axis_index("seq")
    last_cos, last_sin = row_tables(tok_dev)
    back_real = contract("rq,kqc->krc", last_cos, spec_real) - contract(
        "rq,kqc->krc", last_sin, spec_imag
    )
    back_imag = contract("rq,kqc->krc", last_cos, spec_imag) + contract(
        "rq,kqc->krc", last_sin, spec_real
    )
    own_freq = 2 * position + jnp.arange(2, dtype=jnp.int32)
    index_t = jnp.arange(tok_dev, dtype=jnp.int32)
    twist_angle = angles(own_freq[:, None] * index_t[None, :], modulus)
    twist_cos = jnp.cos(twist_angle)[:, :, None]
    twist_sin = jnp.sin(twist_angle)[:, :, None]
    turned_real = back_real * twist_cos - back_imag * twist_sin
    turned_imag = back_real * twist_sin + back_imag * twist_cos
    index_j = jnp.arange(groups, dtype=jnp.int32)
    index_k = jnp.arange(2 * groups, dtype=jnp.int32)
    sum_phase = angles(index_j[:, None] * index_k[None, :], 2 * groups)
    sum_cos = jnp.cos(sum_phase) / modulus
    sum_sin = jnp.sin(sum_phase) / modulus

    def gather_section(pieces):
        real_p, imag_p = pieces
        out_real = contract("jk,krc->jrc", sum_cos, real_p) - contract(
            "jk,krc->jrc", sum_sin, imag_p
        )
        if keep_imag:
            result_imaginary_part = contract("jk,krc->jrc", sum_sin, real_p) + contract(
                "jk,krc->jrc", sum_cos, imag_p
            )
            return jnp.stack([out_real, result_imaginary_part])
        return out_real[None]

    stacked = gather_section(
        (
            lax.all_to_all(turned_real, "seq", split_axis=1, concat_axis=0, tiled=True),
            lax.all_to_all(turned_imag, "seq", split_axis=1, concat_axis=0, tiled=True),
        )
    )
    returned = lax.all_to_all(stacked, "seq", split_axis=1, concat_axis=2, tiled=True)
    return returned.reshape(stacked.shape[0], tok_dev, stacked.shape[3])


def local(signal, gates, filters, skip_gain, out_proj, cotangent):
    channel_count = signal.shape[1]
    seq_total = signal.shape[0] * lax.axis_size("seq")
    spec_real, spec_imag = forward_transform(jnp.concatenate([signal, filters], axis=1))
    sig_real = spec_real[:, :, :channel_count]
    sig_imag = spec_imag[:, :, :channel_count]
    filt_real = spec_real[:, :, channel_count:]
    filt_imag = spec_imag[:, :, channel_count:]
    conv_real = sig_real * filt_real - sig_imag * filt_imag
    conv_imag = sig_real * filt_imag + sig_imag * filt_real
    convolved = inverse_transform(conv_real, conv_imag, False)[0]
    signal_f = signal.astype(jnp.float32)
    gates_f = gates.astype(jnp.float32)
    before_gate = convolved + skip_gain[None, :] * signal_f
    gated = (before_gate * gates_f).astype(jnp.bfloat16)
    weight_rows = lax.all_gather(out_proj, "seq", axis=1, tiled=True)
    partial_sums = jnp.dot(gated, weight_rows, preferred_element_type=jnp.float32)
    mixed = lax.psum_scatter(partial_sums, "chan", scatter_dimension=1, tiled=True).astype(
        jnp.bfloat16
    )
    grad_gated = lax.dot_general(
        lax.all_gather(cotangent, "chan", axis=1, tiled=True),
        weight_rows,
        (((1,), (1,)), ((), ())),
        preferred_element_type=jnp.float32,
    )
    grad_gates = (grad_gated * before_gate).astype(jnp.bfloat16)
    grad_conv = (grad_gated * gates_f).astype(jnp.bfloat16)
    back_real, back_imag = forward_transform(grad_conv)
    first_real = filt_real * back_real + filt_imag * back_imag
    first_imag = filt_real * back_imag - filt_imag * back_real
    second_real = sig_real * back_real + sig_imag * back_imag
    second_imag = sig_real * back_imag - sig_imag * back_real
    result = inverse_transform(first_real - second_imag, first_imag + second_real, True)
    grad_through = result[0]
    grad_kernel = result[1]
    grad_signal = (grad_through + skip_gain[None, :] * grad_conv.astype(jnp.float32)).astype(
        jnp.bfloat16
    )
    grad_filters = (grad_kernel * (1.0 / math.sqrt(seq_total))).astype(jnp.bfloat16)
    return (mixed, grad_signal, grad_gates, grad_filters)


def solution(mesh):
    in_specs = (
        P("seq", "chan"),
        P("seq", "chan"),
        P("seq", "chan"),
        P("chan"),
        P("chan", "seq"),
        P("seq", "chan"),
    )
    out_specs = (P("seq", "chan"), P("seq", "chan"), P("seq", "chan"), P("seq", "chan"))
    return jax.shard_map(local, mesh=mesh, in_specs=in_specs, out_specs=out_specs, check_vma=False)
```

profile of v0, /device:TPU:6, one launch (start us, length us, event | category | flops | bytes accessed | tf_op | source)
XLA Modules:
  0.0 413.3 jit_solution(10535358700498492819)
XLA Ops:
  8.6 1.0 pad_maximum_fusion.1
  10.5 16.6 %all-to-all-start = ((bf16[64,2,1024]{2,1,0:T(2,128)(2,1)}), bf16[64,2,1024]{2,1,0:T(2,128)(2,1)S(1)}, u32[]{:S(2)}, u32[]{:S(2)}) async-start(bf16[64,2,1024]{2,1,0:T(2,128)(2,1)} %reshape.145), calls=%async_computation | async-start | bytes 524288 | tf_op jit(solution)/shard_map/all_to_all | solution.py:39
  27.2 14.8 %all-to-all-done = bf16[64,2,1024]{2,1,0:T(2,128)(2,1)S(1)} async-done(((bf16[64,2,1024]{2,1,0:T(2,128)(2,1)}), bf16[64,2,1024]{2,1,0:T(2,128)(2,1)S(1)}, u32[]{:S(2)}, u32[]{:S(2)}) %all-to-all-start) | async-done | bytes 262176 | tf_op jit(solution)/shard_map/all_to_all | solution.py:39
  42.8 1.0 multiply_add_fusion
  43.8 1.8 copy.50
  45.6 4.7 %all-to-all-start.2 = ((f32[128,2,1024]{2,1,0:T(2,128)}), f32[128,2,1024]{2,1,0:T(2,128)S(1)}, u32[]{:S(2)}, u32[]{:S(2)}) async-start(f32[128,2,1024]{2,1,0:T(2,128)} %copy.50), calls=%async_computation.2 | async-start | bytes 2097152 | tf_op jit(solution)/shard_map/all_to_all | solution.py:48
  50.3 89.6 %all-gather.3.cloned.1.call-done = bf16[512,4096]{0,1:T(8,128)(2,1)} async-done(((bf16[512,64]{0,1:T(8,128)(2,1)}), bf16[512,4096]{0,1:T(8,128)(2,1)}) %all-gather.3.cloned.1.call-update) | async-done | bytes 4194320 | tf_op jit(solution)/shard_map/all_gather | solution.py:120
  139.9 3.2 fusion.8
  143.9 8.7 %all-to-all-start.6 = ((bf16[64,2,512]{2,1,0:T(2,128)(2,1)}), bf16[64,2,512]{2,1,0:T(2,128)(2,1)S(1)}, u32[]{:S(2)}, u32[]{:S(2)}) async-start(bf16[64,2,512]{2,1,0:T(2,128)(2,1)} %reshape.146), calls=%async_computation.7 | async-start | bytes 262144 | tf_op jit(solution)/shard_map/all_to_all | solution.py:39
  152.6 1.8 copy.47
  154.4 10.8 %all-to-all-done.6 = bf16[64,2,512]{2,1,0:T(2,128)(2,1)S(1)} async-done(((bf16[64,2,512]{2,1,0:T(2,128)(2,1)}), bf16[64,2,512]{2,1,0:T(2,128)(2,1)S(1)}, u32[]{:S(2)}, u32[]{:S(2)}) %all-to-all-start.6) | async-done | bytes 131104 | tf_op jit(solution)/shard_map/all_to_all | solution.py:39
  165.2 4.7 %all-to-all-start.1 = ((f32[128,2,1024]{2,1,0:T(2,128)}), f32[128,2,1024]{2,1,0:T(2,128)S(1)}, u32[]{:S(2)}, u32[]{:S(2)}) async-start(f32[128,2,1024]{2,1,0:T(2,128)} %copy.47), calls=%async_computation.1 | async-start | bytes 2097152 | tf_op jit(solution)/shard_map/all_to_all | solution.py:47
  170.4 1.5 multiply_add_fusion.1
  171.9 1.2 copy.65
  173.1 21.9 %all-to-all-done.1 = f32[128,2,1024]{2,1,0:T(2,128)S(1)} async-done(((f32[128,2,1024]{2,1,0:T(2,128)}), f32[128,2,1024]{2,1,0:T(2,128)S(1)}, u32[]{:S(2)}, u32[]{:S(2)}) %all-to-all-start.1) | async-done | bytes 1048608 | tf_op jit(solution)/shard_map/all_to_all | solution.py:47
  195.0 6.9 %all-to-all-start.8 = ((f32[128,2,512]{2,1,0:T(2,128)}), f32[128,2,512]{2,1,0:T(2,128)}, u32[]{:S(2)}, u32[]{:S(2)}) async-start(f32[128,2,512]{2,1,0:T(2,128)} %copy.65), calls=%async_computation.9 | async-start | bytes 1048576 | tf_op jit(solution)/shard_map/all_to_all | solution.py:48
  204.2 1.2 fusion.42
  205.4 2.2 copy.62
  207.6 12.6 %all-to-all-done.8 = f32[128,2,512]{2,1,0:T(2,128)} async-done(((f32[128,2,512]{2,1,0:T(2,128)}), f32[128,2,512]{2,1,0:T(2,128)}, u32[]{:S(2)}, u32[]{:S(2)}) %all-to-all-start.8) | async-done | bytes 524320 | tf_op jit(solution)/shard_map/all_to_all | solution.py:48
  220.3 5.8 %all-to-all-start.7 = ((f32[128,2,512]{2,1,0:T(2,128)}), f32[128,2,512]{2,1,0:T(2,128)}, u32[]{:S(2)}, u32[]{:S(2)}) async-start(f32[128,2,512]{2,1,0:T(2,128)} %copy.62), calls=%async_computation.8 | async-start | bytes 1048576 | tf_op jit(solution)/shard_map/all_to_all | solution.py:47
  226.1 1.2 fusion.44
  227.3 2.2 fusion
  229.5 1.2 fusion.1
  230.8 1.4 copy.66
  232.4 1.6 fusion.34
  234.0 10.4 %all-to-all-done.7 = f32[128,2,512]{2,1,0:T(2,128)} async-done(((f32[128,2,512]{2,1,0:T(2,128)}), f32[128,2,512]{2,1,0:T(2,128)}, u32[]{:S(2)}, u32[]{:S(2)}) %all-to-all-start.7) | async-done | bytes 524320 | tf_op jit(solution)/shard_map/all_to_all | solution.py:47
  244.4 2.1 copy.63
  246.6 1.2 copy.64
  248.6 1.9 fusion.2
  250.5 1.1 subtract_subtract_fusion
  254.9 9.4 %fusion.30 = f32[2,512,128]{2,1,0:T(8,128)S(1)} fusion(f32[2,128,512]{1,2,0:T(8,128)S(1)} %get-tuple-element.5), kind=kOutput, calls=%fused_computation.65 | convolution fusion | flops 201555968 | bytes 1048576 | tf_op jit(solution)/shard_map/rq,kqc->krc/dot_general | solution.py:14
  267.0 1.0 copy.55
  268.0 5.5 %all-to-all-start.3 = ((f32[2,128,512]{2,0,1:T(2,128)}), f32[2,128,512]{2,0,1:T(2,128)S(1)}, u32[]{:S(2)}, u32[]{:S(2)}) async-start(f32[2,128,512]{2,0,1:T(2,128)} %copy.55), calls=%async_computation.3 | async-start | bytes 1048576 | tf_op jit(solution)/shard_map/all_to_all | solution.py:97
  273.5 1.0 copy.57
  274.5 17.2 %all-to-all-done.3 = f32[2,128,512]{2,0,1:T(2,128)S(1)} async-done(((f32[2,128,512]{2,0,1:T(2,128)}), f32[2,128,512]{2,0,1:T(2,128)S(1)}, u32[]{:S(2)}, u32[]{:S(2)}) %all-to-all-start.3) | async-done | bytes 524320 | tf_op jit(solution)/shard_map/all_to_all | solution.py:97
  291.7 5.1 %all-to-all-start.4 = ((f32[2,128,512]{2,0,1:T(2,128)}), f32[2,128,512]{2,0,1:T(2,128)S(1)}, u32[]{:S(2)}, u32[]{:S(2)}) async-start(f32[2,128,512]{2,0,1:T(2,128)} %copy.57), calls=%async_computation.4 | async-start | bytes 1048576 | tf_op jit(solution)/shard_map/all_to_all | solution.py:98
  297.9 16.9 %all-to-all-done.4 = f32[2,128,512]{2,0,1:T(2,128)S(1)} async-done(((f32[2,128,512]{2,0,1:T(2,128)}), f32[2,128,512]{2,0,1:T(2,128)S(1)}, u32[]{:S(2)}, u32[]{:S(2)}) %all-to-all-start.4) | async-done | bytes 524320 | tf_op jit(solution)/shard_map/all_to_all | solution.py:98
  316.7 5.1 %all-to-all-start.5 = ((f32[1,64,2,512]{3,2,0,1:T(2,128)}), f32[1,64,2,512]{3,2,0,1:T(2,128)S(1)}, u32[]{:S(2)}, u32[]{:S(2)}) async-start(f32[1,64,2,512]{3,2,0,1:T(2,128)} %copy.59), calls=%async_computation.5 | async-start | bytes 524288 | tf_op jit(solution)/shard_map/all_to_all | solution.py:101
  321.8 1.0 copy.70
  322.8 12.5 %all-to-all-done.5 = f32[1,64,2,512]{3,2,0,1:T(2,128)S(1)} async-done(((f32[1,64,2,512]{3,2,0,1:T(2,128)}), f32[1,64,2,512]{3,2,0,1:T(2,128)S(1)}, u32[]{:S(2)}, u32[]{:S(2)}) %all-to-all-start.5) | async-done | bytes 262176 | tf_op jit(solution)/shard_map/all_to_all | solution.py:101
  335.3 4.6 %all-to-all-start.9 = ((f32[2,128,512]{2,0,1:T(2,128)}), f32[2,128,512]{2,0,1:T(2,128)S(1)}, u32[]{:S(2)}, u32[]{:S(2)}) async-start(f32[2,128,512]{2,0,1:T(2,128)} %copy.70), calls=%async_computation.10 | async-start | bytes 1048576 | tf_op jit(solution)/shard_map/all_to_all | solution.py:97
  340.2 5.0 %fusion.13 = f32[128,4096]{1,0:T(8,128)} fusion(bf16[512,4096]{0,1:T(8,128)(2,1)} %all-gather.3.cloned.1.call-done, bf16[128,512]{1,0:T(8,128)(2,1)S(1)} %copy-done.3, f32[128,512]{1,0:T(8,128)S(1)} %squeeze_reshape.3, bf16[128,512]{1,0:T(8,128)(2,1)S(1)} %copy-done.1, f32[512]{0:T(512)S(1)} %copy-done.4), kind=kOutput, calls=%fused_computation.46 | convolution fusion | flops 537264128 | bytes 6817792 | tf_op jit(solution)/shard_map/dot_general | solution.py:121
  345.3 1.0 copy.72
  346.3 10.2 %all-to-all-done.9 = f32[2,128,512]{2,0,1:T(2,128)S(1)} async-done(((f32[2,128,512]{2,0,1:T(2,128)}), f32[2,128,512]{2,0,1:T(2,128)S(1)}, u32[]{:S(2)}, u32[]{:S(2)}) %all-to-all-start.9) | async-done | bytes 524320 | tf_op jit(solution)/shard_map/all_to_all | solution.py:97
  356.5 5.4 %all-to-all-start.10 = ((f32[2,128,512]{2,0,1:T(2,128)}), f32[2,128,512]{2,0,1:T(2,128)S(1)}, u32[]{:S(2)}, u32[]{:S(2)}) async-start(f32[2,128,512]{2,0,1:T(2,128)} %copy.72), calls=%async_computation.11 | async-start | bytes 1048576 | tf_op jit(solution)/shard_map/all_to_all | solution.py:98
  362.3 15.8 %all-to-all-done.10 = f32[2,128,512]{2,0,1:T(2,128)S(1)} async-done(((f32[2,128,512]{2,0,1:T(2,128)}), f32[2,128,512]{2,0,1:T(2,128)S(1)}, u32[]{:S(2)}, u32[]{:S(2)}) %all-to-all-start.10) | async-done | bytes 524320 | tf_op jit(solution)/shard_map/all_to_all | solution.py:98
  381.1 21.8 %all_to_all.172 = f32[2,64,2,512]{3,2,0,1:T(2,128)S(1)} all-to-all(f32[2,64,2,512]{3,2,0,1:T(2,128)S(1)} %copy.74), channel_id=1, replica_groups=mesh['seq'=64,'chan'=8] {'seq'}, dimensions={1} | all-to-all | bytes 1048576 | tf_op jit(solution)/shard_map/all_to_all | solution.py:101
  404.9 1.6 convert_element_type.122
  (61 shorter events, 22.0 us)
Async XLA Ops:
  7.2 43.1 %all-gather.5.cloned.1.call-start = ((), (), s32[]{:S(2)}) async-start(), calls=%async_computation.15 | async-start | bytes 1179648 | tf_op jit(solution)/shard_map/all_gather | solution.py:126
  7.9 132.0 %all-gather.3.cloned.1.call-start = ((), (), s32[]{:S(2)}) async-start(), calls=%async_computation.13 | async-start | bytes 4259840 | tf_op jit(solution)/shard_map/all_gather | solution.py:120
  10.5 31.6 %all-to-all-start = ((bf16[64,2,1024]{2,1,0:T(2,128)(2,1)}), bf16[64,2,1024]{2,1,0:T(2,128)(2,1)S(1)}, u32[]{:S(2)}, u32[]{:S(2)}) async-start(bf16[64,2,1024]{2,1,0:T(2,128)(2,1)} %reshape.145), calls=%async_computation | async-start | bytes 524288 | tf_op jit(solution)/shard_map/all_to_all | solution.py:39
  27.2 112.7 %copy-start.2 = (bf16[128,512]{1,0:T(8,128)(2,1)S(1)}, bf16[128,512]{1,0:T(8,128)(2,1)}, u32[]{:S(2)}) copy-start(bf16[128,512]{1,0:T(8,128)(2,1)} %param.7) | copy-start | bytes 393220
  45.6 98.3 %all-to-all-start.2 = ((f32[128,2,1024]{2,1,0:T(2,128)}), f32[128,2,1024]{2,1,0:T(2,128)S(1)}, u32[]{:S(2)}, u32[]{:S(2)}) async-start(f32[128,2,1024]{2,1,0:T(2,128)} %copy.50), calls=%async_computation.2 | async-start | bytes 2097152 | tf_op jit(solution)/shard_map/all_to_all | solution.py:48
  143.9 21.3 %all-to-all-start.6 = ((bf16[64,2,512]{2,1,0:T(2,128)(2,1)}), bf16[64,2,512]{2,1,0:T(2,128)(2,1)S(1)}, u32[]{:S(2)}, u32[]{:S(2)}) async-start(bf16[64,2,512]{2,1,0:T(2,128)(2,1)} %reshape.146), calls=%async_computation.7 | async-start | bytes 262144 | tf_op jit(solution)/shard_map/all_to_all | solution.py:39
  165.2 29.8 %all-to-all-start.1 = ((f32[128,2,1024]{2,1,0:T(2,128)}), f32[128,2,1024]{2,1,0:T(2,128)S(1)}, u32[]{:S(2)}, u32[]{:S(2)}) async-start(f32[128,2,1024]{2,1,0:T(2,128)} %copy.47), calls=%async_computation.1 | async-start | bytes 2097152 | tf_op jit(solution)/shard_map/all_to_all | solution.py:47
  195.0 25.3 %all-to-all-start.8 = ((f32[128,2,512]{2,1,0:T(2,128)}), f32[128,2,512]{2,1,0:T(2,128)}, u32[]{:S(2)}, u32[]{:S(2)}) async-start(f32[128,2,512]{2,1,0:T(2,128)} %copy.65), calls=%async_computation.9 | async-start | bytes 1048576 | tf_op jit(solution)/shard_map/all_to_all | solution.py:48
  220.3 24.2 %all-to-all-start.7 = ((f32[128,2,512]{2,1,0:T(2,128)}), f32[128,2,512]{2,1,0:T(2,128)}, u32[]{:S(2)}, u32[]{:S(2)}) async-start(f32[128,2,512]{2,1,0:T(2,128)} %copy.62), calls=%async_computation.8 | async-start | bytes 1048576 | tf_op jit(solution)/shard_map/all_to_all | solution.py:47
  230.8 19.7 %copy-start = (f32[2,128,1024]{1,2,0:T(8,128)S(1)}, f32[2,128,1024]{1,2,0:T(8,128)}, u32[]{:S(2)}) copy-start(f32[2,128,1024]{1,2,0:T(8,128)} %fusion) | copy-start | bytes 3145732
  268.0 23.7 %all-to-all-start.3 = ((f32[2,128,512]{2,0,1:T(2,128)}), f32[2,128,512]{2,0,1:T(2,128)S(1)}, u32[]{:S(2)}, u32[]{:S(2)}) async-start(f32[2,128,512]{2,0,1:T(2,128)} %copy.55), calls=%async_computation.3 | async-start | bytes 1048576 | tf_op jit(solution)/shard_map/all_to_all | solution.py:97
  291.7 23.1 %all-to-all-start.4 = ((f32[2,128,512]{2,0,1:T(2,128)}), f32[2,128,512]{2,0,1:T(2,128)S(1)}, u32[]{:S(2)}, u32[]{:S(2)}) async-start(f32[2,128,512]{2,0,1:T(2,128)} %copy.57), calls=%async_computation.4 | async-start | bytes 1048576 | tf_op jit(solution)/shard_map/all_to_all | solution.py:98
  296.9 43.3 %copy-start.1 = (bf16[128,512]{1,0:T(8,128)(2,1)S(1)}, bf16[128,512]{1,0:T(8,128)(2,1)}, u32[]{:S(2)}) copy-start(bf16[128,512]{1,0:T(8,128)(2,1)} %param.6) | copy-start | bytes 393220
  296.9 43.3 %copy-start.3 = (bf16[128,512]{1,0:T(8,128)(2,1)S(1)}, bf16[128,512]{1,0:T(8,128)(2,1)}, u32[]{:S(2)}) copy-start(bf16[128,512]{1,0:T(8,128)(2,1)} %param.7) | copy-start | bytes 393220
  296.9 43.3 %copy-start.4 = (f32[512]{0:T(512)S(1)}, f32[512]{0:T(512)}, u32[]{:S(2)}) copy-start(f32[512]{0:T(512)} %param.9) | copy-start | bytes 6148
  316.7 18.6 %all-to-all-start.5 = ((f32[1,64,2,512]{3,2,0,1:T(2,128)}), f32[1,64,2,512]{3,2,0,1:T(2,128)S(1)}, u32[]{:S(2)}, u32[]{:S(2)}) async-start(f32[1,64,2,512]{3,2,0,1:T(2,128)} %copy.59), calls=%async_computation.5 | async-start | bytes 524288 | tf_op jit(solution)/shard_map/all_to_all | solution.py:101
  335.3 21.2 %all-to-all-start.9 = ((f32[2,128,512]{2,0,1:T(2,128)}), f32[2,128,512]{2,0,1:T(2,128)S(1)}, u32[]{:S(2)}, u32[]{:S(2)}) async-start(f32[2,128,512]{2,0,1:T(2,128)} %copy.70), calls=%async_computation.10 | async-start | bytes 1048576 | tf_op jit(solution)/shard_map/all_to_all | solution.py:97
  340.0 64.9 %reduce-scatter.2.cloned.1.call-start = ((), (), s32[]{:S(2)}) async-start(), calls=%async_computation.14 | async-start | bytes 2359296 | tf_op jit(solution)/shard_map/reduce_scatter | solution.py:122
  356.5 21.6 %all-to-all-start.10 = ((f32[2,128,512]{2,0,1:T(2,128)}), f32[2,128,512]{2,0,1:T(2,128)S(1)}, u32[]{:S(2)}, u32[]{:S(2)}) async-start(f32[2,128,512]{2,0,1:T(2,128)} %copy.72), calls=%async_computation.11 | async-start | bytes 1048576 | tf_op jit(solution)/shard_map/all_to_all | solution.py:98
Sparse Core Ops, SparseCore 0:
  10.1 32.0 all-gather.4
  45.2 94.6 all-gather.2
  345.4 36.7 reduce-scatter.1
where the time goes:
time: 418 us; the launch traced here: 413 us
  waiting for transfers between devices  234 us (56%)
  starting transfers between devices  73.1 us (17%)
  matrix products  41.9 us (10%)
  local copies, waits for them, and re-layouts  23.7 us (6%)
  blocking collectives  21.8 us (5%)
  between operations  14.5 us (3%)
    all_gather x1, waiting for transfers between devices, local(): weight_rows = lax.all_gather(out_proj, 'seq', axis=1, tiled=True)  89.6 us
    dot_general x26, matrix products, contract(): return jnp.einsum(spec, table, data, precision=lax.Precision.HIGHEST)  33.7 us
    all_to_all x2, waiting for transfers between devices, inverse_transform(): lax.all_to_all(turned_imag, 'seq', split_axis=1, concat_axis=0, tiled=True)  32.7 us
    all_to_all x2, waiting for transfers between devices, forward_transform(): lax.all_to_all(mid_real, 'seq', split_axis=0, concat_axis=1, tiled=True)  32.3 us
    all_to_all x2, waiting for transfers between devices, inverse_transform(): lax.all_to_all(turned_real, 'seq', split_axis=1, concat_axis=0, tiled=True)  27.4 us
    all_to_all x2, waiting for transfers between devices, forward_transform(): lax.all_to_all(blocks, 'seq', split_axis=0, concat_axis=0, tiled=True)  25.7 us
    all_to_all x2, starting transfers between devices, forward_transform(): lax.all_to_all(blocks, 'seq', split_axis=0, concat_axis=0, tiled=True)  25.3 us
    all_to_all x1, blocking collectives, inverse_transform(): lax.all_to_all(stacked, 'seq', split_axis=1, concat_axis=2, tiled=True)  21.8 us
  transfers between devices with their start and end apart: 14, of which 11 were waited for; matrix products, arithmetic and copies ran while one was open for 10% of the time, Pallas kernels for 0%

commit v1 on v0

v1 whole, which is shorter than its diff:
```python
import functools
import math

import jax
import jax.numpy as jnp
import ml_dtypes
import numpy as np
from jax import lax
from jax.experimental import pallas as pl
from jax.experimental.pallas import tpu as pltpu
from jax.sharding import PartitionSpec as P

LANES = 128
GROUP = 8
CORES = 2
MESH = pl.DeviceIdType.MESH
F32 = jnp.float32
BF16 = jnp.bfloat16


def halves(table):
    high = table.astype(ml_dtypes.bfloat16)
    low = (table - high.astype(np.float64)).astype(ml_dtypes.bfloat16)
    return high, low


def make_tables(blocks):
    total = 2 * blocks * LANES
    rows = -(-(blocks + 1) // 8) * 8
    k = np.arange(rows)
    j = np.arange(blocks)
    b = np.arange(LANES)
    live = (k <= blocks)[:, None].astype(np.float64)
    outer = 2 * np.pi * ((k[:, None] * j[None, :]) % (2 * blocks)) / (2 * blocks)
    first = np.concatenate([live * np.cos(outer), -live * np.sin(outer)], axis=0)
    twist = 2 * np.pi * k[:, None] * b[None, :] / total
    inner = 2 * np.pi * ((b[:, None] * b[None, :]) % LANES) / LANES
    cos, sin = np.cos(inner), np.sin(inner)
    second = np.block([[cos, -sin], [sin, cos]])
    weight = np.where((k == 0) | (k == blocks), 1.0, 2.0)[:, None] * live / total
    last = np.concatenate([weight * np.cos(outer), -weight * np.sin(outer)], axis=0).T
    return (
        np.concatenate(halves(first), axis=1),
        np.stack([np.cos(twist), -np.sin(twist)]).astype(np.float32),
        np.stack(halves(second)),
        np.stack(halves(second.T)),
        np.stack(halves(last)),
    )


def split(value):
    high = value.astype(BF16)
    return high, (value - high.astype(F32)).astype(BF16)


def mm(left, right):
    return jnp.dot(left, right, preferred_element_type=F32)


def forward(x, first, twist, second):
    rows = twist.shape[1]
    mid = mm(first[...], jnp.concatenate([x, x], axis=0))
    cos, sin = twist[0], twist[1]
    pieces = []
    for c in range(GROUP):
        re = mid[:rows, c * LANES : (c + 1) * LANES]
        im = mid[rows:, c * LANES : (c + 1) * LANES]
        pieces.append(jnp.concatenate([re * cos - im * sin, re * sin + im * cos], axis=1))
    high, low = split(jnp.concatenate(pieces, axis=0))
    return mm(high, second[0]) + mm(low, second[0]) + mm(high, second[1])


def inverse(spec, twist, back, last):
    rows = twist.shape[1]
    high, low = split(spec)
    mid = mm(high, back[0]) + mm(low, back[0]) + mm(high, back[1])
    cos, sin = twist[0], twist[1]
    pieces = []
    for c in range(GROUP):
        re = mid[c * rows : (c + 1) * rows, :LANES]
        im = mid[c * rows : (c + 1) * rows, LANES:]
        pieces.append(jnp.concatenate([re * cos + im * sin, im * cos - re * sin], axis=0))
    high, low = split(jnp.concatenate(pieces, axis=1))
    return mm(last[0], high) + mm(last[1], high) + mm(last[0], low)


def times(a, b):
    ar, ai, br, bi = a[:, :LANES], a[:, LANES:], b[:, :LANES], b[:, LANES:]
    return jnp.concatenate([ar * br - ai * bi, ar * bi + ai * br], axis=1)


def times_conj(a, b):
    ar, ai, br, bi = a[:, :LANES], a[:, LANES:], b[:, :LANES], b[:, LANES:]
    return jnp.concatenate([ar * br + ai * bi, ar * bi - ai * br], axis=1)


def kernel(
    ny,
    nz,
    nx,
    sig,
    gat,
    fil,
    skip,
    wgt,
    cot,
    first,
    twist,
    second,
    back,
    last,
    mixed,
    grad_sig,
    grad_gat,
    grad_fil,
    out16,
    in16,
    out8,
    in8,
    gout8,
    gin8,
    rout16,
    rin16,
    rows32,
    sf_spec,
    wt,
    call,
    grad,
    own,
    ex_out,
    ex_in,
    mx_out,
    mx_in,
    a2a_send,
    a2a_recv,
    w_send,
    w_first,
    w_ring,
    c_send,
    c_recv,
    m_send,
    m_recv,
):
    nseq = ny * nz
    chans = GROUP * nseq
    s = lax.axis_index("seq")
    c = lax.axis_index("chan")
    y, z = s // nz, s % nz
    x, core = c // CORES, c % CORES
    sibling = x * CORES + (1 - core)
    block = wgt.shape[1]
    half = block // 2

    def x_peer(dx):
        return ((x + dx) % nx) * CORES + core

    bar = pltpu.get_barrier_semaphore()

    def greet(i, carry):
        pl.semaphore_signal(bar, inc=1, device_id={"seq": (s + i) % nseq}, device_id_type=MESH)
        return carry

    lax.fori_loop(1, nseq, greet, 0)
    for dx in range(1, nx):
        pl.semaphore_signal(bar, inc=1, device_id={"chan": x_peer(dx)}, device_id_type=MESH)
    pl.semaphore_signal(bar, inc=1, device_id={"chan": sibling}, device_id_type=MESH)
    pl.semaphore_wait(bar, nseq + nx - 1)

    def send(src, dst, send_sem, recv_sem, **where):
        pltpu.make_async_remote_copy(
            src_ref=src,
            dst_ref=dst,
            send_sem=send_sem,
            recv_sem=recv_sem,
            device_id=where,
            device_id_type=MESH,
        ).start()

    def wait(ref, sem):
        pltpu.make_async_copy(ref, ref, sem).wait()

    def w_rows(h, yy, zz):
        start = pl.multiple_of((yy * nz + zz) * block + h * half, half)
        return wt.at[pl.ds(start, half)]

    def ring_seq(h, step):
        if h == 0:
            return y * nz + (z + step) % nz
        return ((y + step) % ny) * nz + z

    def ring_block(h, offset, i):
        if h == 0:
            return w_rows(0, (y - i) % ny, (z + offset) % nz)
        return w_rows(1, (y + offset) % ny, (z - i) % nz)

    size = ny
    reach = size // 2

    def pass_on(h, way, d, i):
        sign = 1 if way == 0 else -1
        ref = ring_block(h, -sign * (d - 1), i)
        send(ref, ref, w_send, w_ring.at[h, way, d - 1, i], seq=ring_seq(h, sign))

    def arrived(h, way, d, i):
        sign = 1 if way == 0 else -1
        wait(ring_block(h, -sign * d, i), w_ring.at[h, way, d - 1, i])

    def exists(way, d, parity):
        return d < reach or (d == reach and parity == way)

    def weights_begin():
        def body(n, carry):
            ref = w_rows(0, y, z)
            send(ref, ref, w_send, w_first.at[0, n], seq=((y + n) % ny) * nz + z)
            ref = w_rows(1, y, z)
            send(ref, ref, w_send, w_first.at[1, n], seq=y * nz + (z + n) % nz)
            return carry

        lax.fori_loop(1, size, body, 0)

    def weights_first():
        def body(m, carry):
            for parity in range(2):
                i = 2 * m + parity
                for h in range(2):

                    def landed(i=i, h=h):
                        wait(ring_block(h, 0, i), w_first.at[h, i])

                    if parity == 0:
                        pl.when(m > 0)(landed)
                    else:
                        landed()
                    for way in range(2):
                        if exists(way, 1, parity):
                            pass_on(h, way, 1, i)
            return carry

        lax.fori_loop(0, size // 2, body, 0)

    def weights_step(d):
        def body(m, carry):
            for parity in range(2):
                i = 2 * m + parity
                for h in range(2):
                    for way in range(2):
                        if exists(way, d, parity):
                            arrived(h, way, d, i)
                            if exists(way, d + 1, parity):
                                pass_on(h, way, d + 1, i)
            return carry

        lax.fori_loop(0, size // 2, body, 0)

    def spread(src, dst, n):
        def body(i, carry):
            p = (s + i) % nseq
            send(src.at[p], dst.at[s], a2a_send.at[n], a2a_recv.at[n], seq=p)
            return carry

        lax.fori_loop(1, nseq, body, 0)
        dst[pl.ds(s, 1)] = src[pl.ds(s, 1)]

    def landed(dst, n):
        wait(dst.at[pl.ds(0, nseq - 1)], a2a_recv.at[n])

    mine = pl.multiple_of(s * block, block)
    wt[pl.ds(mine, block), :] = wgt[...].astype(F32).T.astype(BF16)
    weights_begin()

    out16[:, :GROUP, :] = sig[...].astype(F32).T.reshape(nseq, GROUP, LANES).astype(BF16)
    out16[:, GROUP:, :] = fil[...].astype(F32).T.reshape(nseq, GROUP, LANES).astype(BF16)
    spread(out16, in16, 0)

    call[c] = cot[...]
    send(call.at[c], call.at[c], c_send, c_recv.at[0], chan=sibling)
    for dx in range(1, nx):
        send(call.at[c], call.at[c], c_send, c_recv.at[dx], chan=x_peer(dx))

    weights_first()
    for dx in range(1, nx):
        ref = call.at[x_peer(-dx)]
        wait(ref, c_recv.at[dx])
        send(ref, ref, c_send, c_recv.at[nx - 1 + dx], chan=sibling)

    def by_channel(ref, width, start):
        return jnp.concatenate(
            [ref[pl.ds(start + n, nseq, stride=width), :] for n in range(GROUP)], axis=1
        )

    def to_blocks(ref, value, width, start):
        for n in range(GROUP):
            ref[pl.ds(start + n, nseq, stride=width), :] = value[:, n * LANES : (n + 1) * LANES]

    def gain(value):
        return jnp.concatenate(
            [
                value[:, n * LANES : (n + 1) * LANES] * skip[s * GROUP + n]
                for n in range(GROUP)
            ],
            axis=1,
        )

    weights_step(1)

    landed(in16, 0)
    rows32[...] = in16[...].astype(F32).reshape(nseq * 2 * GROUP, LANES)
    sig_x = by_channel(rows32, 2 * GROUP, 0)
    fil_x = by_channel(rows32, 2 * GROUP, GROUP)
    sf_spec[0] = forward(sig_x.astype(BF16), first, twist, second)
    sf_spec[1] = forward(fil_x.astype(BF16), first, twist, second)
    weights_step(2)
    conv = inverse(times(sf_spec[0], sf_spec[1]), twist, back, last)
    to_blocks(rows32, conv + gain(sig_x), GROUP, 0)
    out8[...] = rows32[pl.ds(0, nseq * GROUP), :].reshape(nseq, GROUP, LANES).astype(BF16)
    spread(out8, in8, 1)

    for d in range(3, reach + 1):
        weights_step(d)

    wait(call.at[sibling], c_recv.at[0])
    for dx in range(1, nx):
        wait(call.at[((x - dx) % nx) * CORES + (1 - core)], c_recv.at[nx - 1 + dx])
    total = jnp.zeros((LANES, chans), F32)
    for n in range(nx * CORES):
        total += mm(call[n], wt[pl.ds(n * chans, chans), :])
    grad[...] = total
    gates = gat[...].astype(F32)
    gconv = (total * gates).T
    gout8[...] = gconv.reshape(nseq, GROUP, LANES).astype(BF16)
    spread(gout8, gin8, 2)

    landed(in8, 1)
    before = in8[...].astype(F32).reshape(chans, LANES).T
    grad_gat[...] = (grad[...] * before).astype(BF16)
    gated = (before * gates).astype(BF16)

    def part(n):
        rows = wt[pl.ds(pl.multiple_of(n * chans, chans), chans), :]
        return lax.dot_general(
            gated, rows, (((1,), (1,)), ((), ())), preferred_element_type=F32
        )

    for n in range(nx):
        ex_out[n] = part(n * CORES + (1 - core)).astype(BF16)
        send(ex_out.at[n], ex_in.at[n], m_send.at[0], m_recv.at[n], chan=sibling)
    for n in range(nx):
        own[n] = part(n * CORES + core)

    landed(gin8, 2)
    rows32[pl.ds(0, nseq * GROUP), :] = gin8[...].astype(F32).reshape(nseq * GROUP, LANES)
    grad_x = by_channel(rows32, GROUP, 0)
    g_spec = forward(grad_x.astype(BF16), first, twist, second)
    through = inverse(times_conj(sf_spec[1], g_spec), twist, back, last)
    kern = inverse(times_conj(sf_spec[0], g_spec), twist, back, last)
    to_blocks(rows32, through + gain(grad_x), 2 * GROUP, 0)
    to_blocks(rows32, kern * (1.0 / math.sqrt(nseq * LANES)), 2 * GROUP, GROUP)
    rout16[...] = rows32[...].reshape(nseq, 2 * GROUP, LANES).astype(BF16)
    spread(rout16, rin16, 3)

    for n in range(nx):
        wait(ex_in.at[n], m_recv.at[n])
        own[n] += ex_in[n].astype(F32)
    for dx in range(1, nx):
        mx_out[dx - 1] = own[(x + dx) % nx].astype(BF16)
        send(mx_out.at[dx - 1], mx_in.at[dx - 1], m_send.at[1], m_recv.at[nx + dx], chan=x_peer(dx))
    result = own[x]
    for dx in range(1, nx):
        wait(mx_in.at[dx - 1], m_recv.at[nx + dx])
        result += mx_in[dx - 1].astype(F32)
    mixed[...] = result.astype(BF16)

    landed(rin16, 3)
    grads = rin16[...].astype(F32)
    grad_sig[...] = grads[:, :GROUP, :].reshape(chans, LANES).T.astype(BF16)
    grad_fil[...] = grads[:, GROUP:, :].reshape(chans, LANES).T.astype(BF16)

    for n, src in enumerate((out16, out8, gout8, rout16)):
        wait(src.at[pl.ds(0, nseq - 1)], a2a_send.at[n])
    wait(wt.at[pl.ds(0, (nseq - 1) * block)], w_send)
    wait(call.at[pl.ds(0, 2 * nx - 1)], c_send)
    wait(ex_out, m_send.at[0])
    wait(mx_out, m_send.at[1])


def local(ny, nz, nx, signal, gates, filters, skip_gain, out_proj, cotangent):
    nseq = ny * nz
    chans = signal.shape[1]
    block = out_proj.shape[1]
    first, twist, second, back, last = make_tables(nseq)
    rows = twist.shape[1]
    vmem = pl.BlockSpec(memory_space=pltpu.VMEM)
    smem = pl.BlockSpec(memory_space=pltpu.SMEM)
    out = jax.ShapeDtypeStruct((LANES, chans), BF16)
    wide = (nseq, 2 * GROUP, LANES)
    narrow = (nseq, GROUP, LANES)
    tile = (LANES, chans)
    return pl.pallas_call(
        functools.partial(kernel, ny, nz, nx),
        out_shape=[out] * 4,
        in_specs=[vmem, vmem, vmem, smem] + [vmem] * 7,
        out_specs=[vmem] * 4,
        scratch_shapes=[
            pltpu.VMEM(wide, BF16),
            pltpu.VMEM(wide, BF16),
            pltpu.VMEM(narrow, BF16),
            pltpu.VMEM(narrow, BF16),
            pltpu.VMEM(narrow, BF16),
            pltpu.VMEM(narrow, BF16),
            pltpu.VMEM(wide, BF16),
            pltpu.VMEM(wide, BF16),
            pltpu.VMEM((nseq * 2 * GROUP, LANES), F32),
            pltpu.VMEM((2, GROUP * rows, 2 * LANES), F32),
            pltpu.VMEM((nseq * block, chans), BF16),
            pltpu.VMEM((nx * CORES,) + tile, BF16),
            pltpu.VMEM(tile, F32),
            pltpu.VMEM((nx,) + tile, F32),
            pltpu.VMEM((nx,) + tile, BF16),
            pltpu.VMEM((nx,) + tile, BF16),
            pltpu.VMEM((nx - 1,) + tile, BF16),
            pltpu.VMEM((nx - 1,) + tile, BF16),
            pltpu.SemaphoreType.DMA((4,)),
            pltpu.SemaphoreType.DMA((4,)),
            pltpu.SemaphoreType.DMA,
            pltpu.SemaphoreType.DMA((2, ny)),
            pltpu.SemaphoreType.DMA((2, 2, ny // 2, ny)),
            pltpu.SemaphoreType.DMA,
            pltpu.SemaphoreType.DMA((2 * nx,)),
            pltpu.SemaphoreType.DMA((2,)),
            pltpu.SemaphoreType.DMA((2 * nx,)),
        ],
        compiler_params=pltpu.CompilerParams(
            collective_id=0, has_side_effects=True, vmem_limit_bytes=48 * 1024 * 1024
        ),
    )(signal, gates, filters, skip_gain, out_proj, cotangent, first, twist, second, back, last)


def solution(mesh):
    side = math.isqrt(mesh.shape["seq"])
    nx = mesh.shape["chan"] // CORES
    in_specs = (
        P("seq", "chan"),
        P("seq", "chan"),
        P("seq", "chan"),
        P("chan"),
        P("chan", "seq"),
        P("seq", "chan"),
    )
    out_specs = (P("seq", "chan"),) * 4
    return jax.shard_map(
        functools.partial(local, side, side, nx),
        mesh=mesh,
        in_specs=in_specs,
        out_specs=out_specs,
        check_vma=False,
    )
```

time: 418 us -> 86 us (0.21); the launches traced: 413 us -> 85.6 us
  waiting for transfers between devices: 234 us -> 0 us
  Pallas kernels: 0 us -> 74.3 us
  starting transfers between devices: 73.1 us -> 0 us
  matrix products: 41.9 us -> 0 us
  blocking collectives: 21.8 us -> 0 us
  between operations: 14.5 us -> 0.69 us
  local copies, waits for them, and re-layouts: 23.7 us -> 10.6 us
    all_to_all x11 -> x0, waiting for transfers between devices: 143 us -> none  [the longest x2 32.7 us: inverse_transform(): lax.all_to_all(turned_imag, 'seq', split_axis=1, concat_axis=0, tiled=True)]
    all_gather x2 -> x0, waiting for transfers between devices: 89.7 us -> none  [the longest x1 89.6 us: local(): weight_rows = lax.all_gather(out_proj, 'seq', axis=1, tiled=True)]
    pallas_call x0 -> x1, Pallas kernels: none -> 74.3 us  [local(): pl.pallas_call(functools.partial(kernel, ny, nz, nx), out_shape=[out] * 4...]
    all_to_all x11 -> x0, starting transfers between devices: 73 us -> none  [the longest x2 25.3 us: forward_transform(): lax.all_to_all(blocks, 'seq', split_axis=0, concat_axis=0, tiled=True)]
    dot_general x28 -> x0, matrix products: 41.9 us -> none  [the longest x26 33.7 us: contract(): return jnp.einsum(spec, table, data, precision=lax.Precision.HIGHEST)]
    all_to_all x1 -> x0, blocking collectives: 21.8 us -> none  [inverse_transform(): lax.all_to_all(stacked, 'seq', split_axis=1, concat_axis=2, tiled=True)]
    unnamed x10 -> x25, local copies, waits for them, and re-layouts: 0.03 us -> 10.6 us
    all_to_all x16 -> x0, local copies, waits for them, and re-layouts: 8.65 us -> none  [the longest x4 4.39 us: forward_transform(): lax.all_to_all(mid_real, 'seq', split_axis=0, concat_axis=1, tiled=True)]
  transfers between devices with their start and end apart: 14 -> 0, of which waited for: 11 -> 0; matrix products, arithmetic and copies ran while one was open for 10% -> 0% of each run, Pallas kernels for 0% -> 0%
where the time goes in v1:
time: 86 us; the launch traced here: 85.6 us
  Pallas kernels  74.3 us (86%)
  local copies, waits for them, and re-layouts  10.6 us (12%)
    pallas_call x1, Pallas kernels, local(): pl.pallas_call(functools.partial(kernel, ny, nz, nx), out_shape=[out] * 4...  74.3 us
    unnamed x25, local copies, waits for them, and re-layouts  10.6 us

profile of v1, /device:TPU:6, one launch (start us, length us, event | category | flops | bytes accessed | tf_op | source)
XLA Modules:
  0.0 85.6 jit_solution(13451672350452127350)
XLA Ops:
  0.6 0.0 copy-start.7
  0.6 0.0 copy-start.2
  0.7 1.0 %copy.15.wgt = bf16[512,64]{1,0:T(8,128)(2,1)S(1)} copy(bf16[512,64]{0,1:T(8,128)(2,1)} %param.15) | data formatting | bytes 131072 | tf_op args[4]
  1.7 0.0 copy-done.7
  1.7 0.0 copy-done.2
  1.7 0.0 copy-start
  1.7 0.9 %copy-done = bf16[2,256,256]{2,1,0:T(8,128)(2,1)S(1)} copy-done((bf16[2,256,256]{2,1,0:T(8,128)(2,1)S(1)}, bf16[2,256,256]{2,1,0:T(8,128)(2,1)}, u32[]{:S(2)}) %copy-start) | copy-done | bytes 262168
  2.6 0.0 copy-start.1
  2.6 0.9 %copy-done.1 = bf16[2,256,256]{2,1,0:T(8,128)(2,1)S(1)} copy-done((bf16[2,256,256]{2,1,0:T(8,128)(2,1)S(1)}, bf16[2,256,256]{2,1,0:T(8,128)(2,1)}, u32[]{:S(2)}) %copy-start.1) | copy-done | bytes 262168
  3.6 0.0 copy-start.3
  3.6 0.9 %copy-done.3 = bf16[128,512]{1,0:T(8,128)(2,1)S(1)} copy-done((bf16[128,512]{1,0:T(8,128)(2,1)S(1)}, bf16[128,512]{1,0:T(8,128)(2,1)}, u32[]{:S(2)}) %copy-start.3) | copy-done | bytes 131096
  4.5 0.0 copy-start.4
  4.5 0.9 %copy-done.4 = bf16[128,512]{1,0:T(8,128)(2,1)S(1)} copy-done((bf16[128,512]{1,0:T(8,128)(2,1)S(1)}, bf16[128,512]{1,0:T(8,128)(2,1)}, u32[]{:S(2)}) %copy-start.4) | copy-done | bytes 131096
  5.4 0.0 copy-start.5
  5.4 0.9 %copy-done.5 = bf16[128,512]{1,0:T(8,128)(2,1)S(1)} copy-done((bf16[128,512]{1,0:T(8,128)(2,1)S(1)}, bf16[128,512]{1,0:T(8,128)(2,1)}, u32[]{:S(2)}) %copy-start.5) | copy-done | bytes 131096
  6.3 0.0 copy-start.6
  6.3 0.9 %copy-done.6 = f32[2,72,128]{2,1,0:T(8,128)S(1)} copy-done((f32[2,72,128]{2,1,0:T(8,128)S(1)}, f32[2,72,128]{2,1,0:T(8,128)}, u32[]{:S(2)}) %copy-start.6) | copy-done | bytes 73752
  7.2 0.0 copy-start.8
  7.2 0.8 copy-done.8
  7.9 0.0 copy-start.9
  7.9 0.7 copy-done.9
  8.6 74.3 %shard_map.138 = (bf16[128,512]{1,0:T(8,128)(2,1)S(1)}, bf16[128,512]{1,0:T(8,128)(2,1)S(1)}, bf16[128,512]{1,0:T(8,128)(2,1)S(1)}, bf16[128,512]{1,0:T(8,128)(2,1)S(1)}) custom-call(bf16[128,512]{1,0:T(8,128)(2,1)S(1)} %copy-done.2, bf16[128,512]{1,0:T(8,128)(2,1)S(1)} %copy-done.3, bf16[128,512]{1,0:T(8,128)(2,1)S(1)} %copy-done.4, f32[512]{0:T(512)S(1)} %copy-done.9, ...), custom_call_target="tpu_custom_call" | custom-call | tf_op jit(solution)/shard_map/pallas_call | solution.py:398
  82.9 0.7 copy.20
  83.6 0.7 copy.21
  84.2 0.7 copy.22
  84.9 0.7 copy.23
Async XLA Ops:
  0.6 1.0 %copy-start.7 = (bf16[2,64,144]{2,1,0:T(8,128)(2,1)S(1)}, bf16[2,64,144]{2,1,0:T(8,128)(2,1)}, u32[]{:S(2)}) copy-start(bf16[2,64,144]{2,1,0:T(8,128)(2,1)} %constant.14.clone.last) | copy-start | bytes 110596
  0.6 1.0 %copy-start.2 = (bf16[128,512]{1,0:T(8,128)(2,1)S(1)}, bf16[128,512]{1,0:T(8,128)(2,1)}, u32[]{:S(2)}) copy-start(bf16[128,512]{1,0:T(8,128)(2,1)} %sig.1) | copy-start | bytes 393220
  1.7 1.0 %copy-start = (bf16[2,256,256]{2,1,0:T(8,128)(2,1)S(1)}, bf16[2,256,256]{2,1,0:T(8,128)(2,1)}, u32[]{:S(2)}) copy-start(bf16[2,256,256]{2,1,0:T(8,128)(2,1)} %constant.13.clone.back) | copy-start | bytes 786436
  2.6 0.9 %copy-start.1 = (bf16[2,256,256]{2,1,0:T(8,128)(2,1)S(1)}, bf16[2,256,256]{2,1,0:T(8,128)(2,1)}, u32[]{:S(2)}) copy-start(bf16[2,256,256]{2,1,0:T(8,128)(2,1)} %constant.12.clone.second) | copy-start | bytes 786436
  3.6 0.9 %copy-start.3 = (bf16[128,512]{1,0:T(8,128)(2,1)S(1)}, bf16[128,512]{1,0:T(8,128)(2,1)}, u32[]{:S(2)}) copy-start(bf16[128,512]{1,0:T(8,128)(2,1)} %gat.1) | copy-start | bytes 393220
  4.5 0.9 %copy-start.4 = (bf16[128,512]{1,0:T(8,128)(2,1)S(1)}, bf16[128,512]{1,0:T(8,128)(2,1)}, u32[]{:S(2)}) copy-start(bf16[128,512]{1,0:T(8,128)(2,1)} %fil.1) | copy-start | bytes 393220
  5.4 0.9 %copy-start.5 = (bf16[128,512]{1,0:T(8,128)(2,1)S(1)}, bf16[128,512]{1,0:T(8,128)(2,1)}, u32[]{:S(2)}) copy-start(bf16[128,512]{1,0:T(8,128)(2,1)} %cot.1) | copy-start | bytes 393220
  6.3 0.9 %copy-start.6 = (f32[2,72,128]{2,1,0:T(8,128)S(1)}, f32[2,72,128]{2,1,0:T(8,128)}, u32[]{:S(2)}) copy-start(f32[2,72,128]{2,1,0:T(8,128)} %constant.11.clone.twist) | copy-start | bytes 221188
  7.2 0.8 copy-start.8
  7.9 0.7 copy-start.9

commit v2 on v1

--- a/solution.py
+++ b/solution.py
@@ -14,6 +14,7 @@
 GROUP = 8
 CORES = 2
 MESH = pl.DeviceIdType.MESH
+VMEM_LIMIT = 60 * 1024 * 1024
 F32 = jnp.float32
 BF16 = jnp.bfloat16
 
@@ -98,21 +99,27 @@
     ny,
     nz,
     nx,
+    skip,
+    sig_hbm,
+    gat_hbm,
+    fil_hbm,
+    wgt_hbm,
+    cot_hbm,
+    first_hbm,
+    twist_hbm,
+    second_hbm,
+    back_hbm,
+    last_hbm,
+    outs,
     sig,
     gat,
     fil,
-    skip,
-    wgt,
-    cot,
     first,
     twist,
     second,
     back,
     last,
-    mixed,
-    grad_sig,
-    grad_gat,
-    grad_fil,
+    load_sem,
     out16,
     in16,
     out8,
@@ -140,6 +147,7 @@
     c_recv,
     m_send,
     m_recv,
+    all_in,
 ):
     nseq = ny * nz
     chans = GROUP * nseq
@@ -148,23 +156,59 @@
     y, z = s // nz, s % nz
     x, core = c // CORES, c % CORES
     sibling = x * CORES + (1 - core)
-    block = wgt.shape[1]
+    block = wgt_hbm.shape[0]
     half = block // 2
 
     def x_peer(dx):
         return ((x + dx) % nx) * CORES + core
 
+    mine = pl.ds(pl.multiple_of(s * block, block), block)
+    loads = [
+        pltpu.make_async_copy(src, dst, load_sem.at[n])
+        for n, (src, dst) in enumerate(
+            (
+                (wgt_hbm, wt.at[mine]),
+                (sig_hbm, sig),
+                (fil_hbm, fil),
+                (cot_hbm, call.at[c]),
+                (gat_hbm, gat),
+                (first_hbm, first),
+                (twist_hbm, twist),
+                (second_hbm, second),
+                (back_hbm, back),
+                (last_hbm, last),
+            )
+        )
+    ]
+    for load in loads:
+        load.start()
+
     bar = pltpu.get_barrier_semaphore()
 
-    def greet(i, carry):
-        pl.semaphore_signal(bar, inc=1, device_id={"seq": (s + i) % nseq}, device_id_type=MESH)
+    def row_peer(n):
+        return y * nz + (z + n) % nz
+
+    def column_peer(n):
+        return ((y + n) % ny) * nz + z
+
+    def greet(n, carry):
+        for peer in (row_peer(n), column_peer(n)):
+            pl.semaphore_signal(bar, inc=1, device_id={"seq": peer}, device_id_type=MESH)
         return carry
 
-    lax.fori_loop(1, nseq, greet, 0)
+    lax.fori_loop(1, ny, greet, 0)
     for dx in range(1, nx):
         pl.semaphore_signal(bar, inc=1, device_id={"chan": x_peer(dx)}, device_id_type=MESH)
     pl.semaphore_signal(bar, inc=1, device_id={"chan": sibling}, device_id_type=MESH)
-    pl.semaphore_wait(bar, nseq + nx - 1)
+    pl.semaphore_wait(bar, ny + nz + nx - 2)
+
+    def greet_all(n, carry):
+        pl.semaphore_signal(
+            all_in, inc=1, device_id={"seq": row_peer(n)}, device_id_type=MESH
+        )
+        return carry
+
+    lax.fori_loop(1, nz, greet_all, 0)
 
     def send(src, dst, send_sem, recv_sem, **where):
         pltpu.make_async_remote_copy(
@@ -264,19 +308,23 @@
     def landed(dst, n):
         wait(dst.at[pl.ds(0, nseq - 1)], a2a_recv.at[n])
 
-    mine = pl.multiple_of(s * block, block)
-    wt[pl.ds(mine, block), :] = wgt[...].astype(F32).T.astype(BF16)
+    loads[0].wait()
     weights_begin()
+    loads[1].wait()
+    loads[2].wait()
 
     out16[:, :GROUP, :] = sig[...].astype(F32).T.reshape(nseq, GROUP, LANES).astype(BF16)
     out16[:, GROUP:, :] = fil[...].astype(F32).T.reshape(nseq, GROUP, LANES).astype(BF16)
+    pl.semaphore_wait(all_in, nz - 1)
     spread(out16, in16, 0)
 
-    call[c] = cot[...]
+    loads[3].wait()
     send(call.at[c], call.at[c], c_send, c_recv.at[0], chan=sibling)
     for dx in range(1, nx):
         send(call.at[c], call.at[c], c_send, c_recv.at[dx], chan=x_peer(dx))
 
+    for load in loads[4:]:
+        load.wait()
     weights_first()
     for dx in range(1, nx):
         ref = call.at[x_peer(-dx)]
@@ -332,7 +380,7 @@
 
     landed(in8, 1)
     before = in8[...].astype(F32).reshape(chans, LANES).T
-    grad_gat[...] = (grad[...] * before).astype(BF16)
+    outs[2] = (grad[...] * before).astype(BF16)
     gated = (before * gates).astype(BF16)
 
     def part(n):
@@ -368,12 +416,12 @@
     for dx in range(1, nx):
         wait(mx_in.at[dx - 1], m_recv.at[nx + dx])
         result += mx_in[dx - 1].astype(F32)
-    mixed[...] = result.astype(BF16)
+    outs[0] = result.astype(BF16)
 
     landed(rin16, 3)
     grads = rin16[...].astype(F32)
-    grad_sig[...] = grads[:, :GROUP, :].reshape(chans, LANES).T.astype(BF16)
-    grad_fil[...] = grads[:, GROUP:, :].reshape(chans, LANES).T.astype(BF16)
+    outs[1] = grads[:, :GROUP, :].reshape(chans, LANES).T.astype(BF16)
+    outs[3] = grads[:, GROUP:, :].reshape(chans, LANES).T.astype(BF16)
 
     for n, src in enumerate((out16, out8, gout8, rout16)):
         wait(src.at[pl.ds(0, nseq - 1)], a2a_send.at[n])
@@ -389,18 +437,28 @@
     block = out_proj.shape[1]
     first, twist, second, back, last = make_tables(nseq)
     rows = twist.shape[1]
+    hbm = pl.BlockSpec(memory_space=pltpu.HBM)
     vmem = pl.BlockSpec(memory_space=pltpu.VMEM)
     smem = pl.BlockSpec(memory_space=pltpu.SMEM)
     out = jax.ShapeDtypeStruct((LANES, chans), BF16)
     wide = (nseq, 2 * GROUP, LANES)
     narrow = (nseq, GROUP, LANES)
     tile = (LANES, chans)
-    return pl.pallas_call(
+    results = pl.pallas_call(
         functools.partial(kernel, ny, nz, nx),
-        out_shape=[out] * 4,
-        in_specs=[vmem, vmem, vmem, smem] + [vmem] * 7,
-        out_specs=[vmem] * 4,
+        out_shape=jax.ShapeDtypeStruct((4, LANES, chans), BF16),
+        in_specs=[smem] + [hbm] * 10,
+        out_specs=vmem,
         scratch_shapes=[
+            pltpu.VMEM(tile, BF16),
+            pltpu.VMEM(tile, BF16),
+            pltpu.VMEM(tile, BF16),
+            pltpu.VMEM(first.shape, BF16),
+            pltpu.VMEM(twist.shape, F32),
+            pltpu.VMEM(second.shape, BF16),
+            pltpu.VMEM(back.shape, BF16),
+            pltpu.VMEM(last.shape, BF16),
+            pltpu.SemaphoreType.DMA((10,)),
             pltpu.VMEM(wide, BF16),
             pltpu.VMEM(wide, BF16),
             pltpu.VMEM(narrow, BF16),
@@ -428,11 +486,25 @@
             pltpu.SemaphoreType.DMA((2 * nx,)),
             pltpu.SemaphoreType.DMA((2,)),
             pltpu.SemaphoreType.DMA((2 * nx,)),
+            pltpu.SemaphoreType.REGULAR,
         ],
         compiler_params=pltpu.CompilerParams(
-            collective_id=0, has_side_effects=True, vmem_limit_bytes=48 * 1024 * 1024
+            collective_id=0, has_side_effects=True, vmem_limit_bytes=VMEM_LIMIT
         ),
-    )(signal, gates, filters, skip_gain, out_proj, cotangent, first, twist, second, back, last)
+    )(
+        skip_gain,
+        signal,
+        gates,
+        filters,
+        out_proj.T,
+        cotangent,
+        first,
+        twist,
+        second,
+        back,
+        last,
+    )
+    return tuple(results[n] for n in range(4))
 
 
 def solution(mesh):

time: 86 us -> 76.6 us (0.89)
  local copies, waits for them, and re-layouts: 10.6 us -> 1.89 us
  Pallas kernels: 74.3 us -> 73.4 us
    unnamed x25 -> x0, local copies, waits for them, and re-layouts: 10.6 us -> none
    squeeze x0 -> x1, local copies, waits for them, and re-layouts: none -> 1.89 us  [local(): return tuple((results[n] for n in range(4)))]
where the time goes in v2:
time: 76.6 us; the launch traced here: 76 us
  Pallas kernels  73.4 us (96%)
  local copies, waits for them, and re-layouts  1.89 us (2%)
    pallas_call x1, Pallas kernels, local(): pl.pallas_call(functools.partial(kernel, ny, nz, nx), out_shape=jax.Shape...  73.4 us
    squeeze x1, local copies, waits for them, and re-layouts, local(): return tuple((results[n] for n in range(4)))  1.89 us

profile of v2, /device:TPU:6, one launch (start us, length us, event | category | flops | bytes accessed | tf_op | source)
XLA Modules:
  0.0 76.0 jit_solution(7002608728028964709)
XLA Ops:
  0.6 73.4 %shard_map.138 = bf16[4,128,512]{2,1,0:T(8,128)(2,1)} custom-call(f32[512]{0:T(512)} %skip.1, bf16[128,512]{1,0:T(8,128)(2,1)} %sig_hbm.1, bf16[128,512]{1,0:T(8,128)(2,1)} %gat_hbm.1, bf16[128,512]{1,0:T(8,128)(2,1)} %fil_hbm.1, bf16[64,512]{1,0:T(8,128)(2,1)} %bitcast.9, bf16[128,512]{1,0:T(8,128)(2,1)} %cot_hbm.1, ...), custom_call_target="tpu_custom_call" | custom-call | tf_op jit(solution)/shard_map/pallas_call | solution.py:447
  74.1 1.9 %slice_bitcast_fusion = (bf16[128,512]{1,0:T(8,128)(2,1)}, bf16[128,512]{1,0:T(8,128)(2,1)}, bf16[128,512]{1,0:T(8,128)(2,1)}, bf16[128,512]{1,0:T(8,128)(2,1)}) fusion(bf16[4,128,512]{2,1,0:T(8,128)(2,1)} %shard_map.138), kind=kLoop, calls=%fused_computation | loop fusion | bytes 1048576 | tf_op jit(solution)/shard_map/squeeze | solution.py:507

commit v3 on v2

--- a/solution.py
+++ b/solution.py
@@ -131,22 +131,45 @@
     rows32,
     sf_spec,
     wt,
-    call,
-    grad,
-    own,
-    ex_out,
-    ex_in,
-    mx_out,
-    mx_in,
+    order,
+    cot_own,
+    cot_perm,
+    ck0,
+    ck1,
+    gp_out,
+    gp_in,
+    gated,
+    own0,
+    own1,
+    ex0_out,
+    ex0_in,
+    ex1_out,
+    ex1_in,
+    mx0_out,
+    mx0_in,
+    mx1_out,
+    mx1_in,
+    ret0_out,
+    ret0_in,
+    ret1_out,
+    ret1_in,
+    perm,
+    gating,
     a2a_send,
     a2a_recv,
     w_send,
     w_first,
     w_ring,
-    c_send,
-    c_recv,
-    m_send,
-    m_recv,
+    k0_send,
+    k0_recv,
+    k1_send,
+    k1_recv,
+    p_send,
+    p_recv,
+    m0_send,
+    m0_recv,
+    m1_send,
+    m1_recv,
     all_in,
 ):
     nseq = ny * nz
@@ -158,19 +181,43 @@
     sibling = x * CORES + (1 - core)
     block = wgt_hbm.shape[0]
     half = block // 2
+    quarter = chans // 4
+    middle = chans // 2
+    pz, py = z % 2, y % 2
+    z_pair = y * nz + (z + 1 - 2 * pz)
+    y_pair = (y + 1 - 2 * py) * nz + z
+    keeps = core == py
+    hop = ny // 2
+    base = nseq * half // 2
+
+    def cols0(n):
+        return pl.ds(pl.multiple_of(n * quarter, quarter), quarter)
+
+    def cols1(n):
+        return pl.ds(pl.multiple_of(n * middle, middle), middle)
 
     def x_peer(dx):
         return ((x + dx) % nx) * CORES + core
 
-    mine = pl.ds(pl.multiple_of(s * block, block), block)
+    def w_rows(h, a, b):
+        width = nz // 2 if h == 0 else nz
+        start = pl.multiple_of(h * base + (a * width + b) * half, half)
+        return wt.at[pl.ds(start, half)]
+
+    def held(h, i, d):
+        if h == 0:
+            return w_rows(0, (y - d) % ny, (z // 2 - i) % hop)
+        return w_rows(1, (y // 2 - i) % hop, (z - d) % nz)
+
     loads = [
         pltpu.make_async_copy(src, dst, load_sem.at[n])
         for n, (src, dst) in enumerate(
             (
-                (wgt_hbm, wt.at[mine]),
+                (wgt_hbm.at[pl.ds(0, half)], held(0, 0, 0)),
+                (wgt_hbm.at[pl.ds(half, half)], held(1, 0, 0)),
+                (cot_hbm, cot_own),
                 (sig_hbm, sig),
                 (fil_hbm, fil),
-                (cot_hbm, call.at[c]),
                 (gat_hbm, gat),
                 (first_hbm, first),
                 (twist_hbm, twist),
@@ -200,6 +247,31 @@
     for dx in range(1, nx):
         pl.semaphore_signal(bar, inc=1, device_id={"chan": x_peer(dx)}, device_id_type=MESH)
     pl.semaphore_signal(bar, inc=1, device_id={"chan": sibling}, device_id_type=MESH)
+
+    loads[3].wait()
+    loads[4].wait()
+    out16[:, :GROUP, :] = sig[...].astype(F32).T.reshape(nseq, GROUP, LANES).astype(BF16)
+    out16[:, GROUP:, :] = fil[...].astype(F32).T.reshape(nseq, GROUP, LANES).astype(BF16)
+    column = lax.broadcasted_iota(jnp.int32, (chans, chans), 0)
+    place = lax.broadcasted_iota(jnp.int32, (chans, chans), 1)
+    zz = column // block
+    rest = column % block
+    target = jnp.where(
+        rest < half,
+        (zz % 2) * quarter + (zz // 2) * half + rest,
+        middle + zz * half + rest - half,
+    )
+    order[...] = (place == target).astype(F32).astype(BF16)
+    loads[2].wait()
+    cot_perm[...] = mm(cot_own[...], order[...]).astype(BF16)
+    near = pl.ds(pl.multiple_of(pz * quarter, quarter), quarter)
+    far = pl.ds(pl.multiple_of((1 - pz) * quarter, quarter), quarter)
+    ck0[0, :, cols0(c)] = cot_perm[:, near]
+
+    @pl.when(keeps)
+    def _():
+        ck1[0, :, cols1(x)] = cot_perm[:, middle:]
+
     pl.semaphore_wait(bar, ny + nz + nx - 2)
 
     def greet_all(n, carry):
@@ -223,113 +295,65 @@
     def wait(ref, sem):
         pltpu.make_async_copy(ref, ref, sem).wait()
 
-    def w_rows(h, yy, zz):
-        start = pl.multiple_of((yy * nz + zz) * block + h * half, half)
-        return wt.at[pl.ds(start, half)]
-
-    def ring_seq(h, step):
-        if h == 0:
-            return y * nz + (z + step) % nz
-        return ((y + step) % ny) * nz + z
-
-    def ring_block(h, offset, i):
-        if h == 0:
-            return w_rows(0, (y - i) % ny, (z + offset) % nz)
-        return w_rows(1, (y + offset) % ny, (z - i) % nz)
-
-    size = ny
-    reach = size // 2
+    reach = ny // 2
+
+    def beside(h, way):
+        step = 1 - 2 * way
+        return column_peer(step) if h == 0 else row_peer(step)
 
     def pass_on(h, way, d, i):
-        sign = 1 if way == 0 else -1
-        ref = ring_block(h, -sign * (d - 1), i)
-        send(ref, ref, w_send, w_ring.at[h, way, d - 1, i], seq=ring_seq(h, sign))
-
-    def arrived(h, way, d, i):
-        sign = 1 if way == 0 else -1
-        wait(ring_block(h, -sign * d, i), w_ring.at[h, way, d - 1, i])
+        sign = 1 - 2 * way
+        ref = held(h, i, sign * (d - 1))
+        send(ref, ref, w_send, w_ring.at[h, way, d - 1, i], seq=beside(h, way))
 
     def exists(way, d, parity):
         return d < reach or (d == reach and parity == way)
 
     def weights_begin():
         def body(n, carry):
-            ref = w_rows(0, y, z)
-            send(ref, ref, w_send, w_first.at[0, n], seq=((y + n) % ny) * nz + z)
-            ref = w_rows(1, y, z)
-            send(ref, ref, w_send, w_first.at[1, n], seq=y * nz + (z + n) % nz)
+            ref = held(0, 0, 0)
+            send(ref, ref, w_send, w_first.at[0, n], seq=row_peer(2 * n))
+            ref = held(1, 0, 0)
+            send(ref, ref, w_send, w_first.at[1, n], seq=column_peer(2 * n))
             return carry
 
-        lax.fori_loop(1, size, body, 0)
-
-    def weights_first():
-        def body(m, carry):
-            for parity in range(2):
-                i = 2 * m + parity
-                for h in range(2):
-
-                    def landed(i=i, h=h):
-                        wait(ring_block(h, 0, i), w_first.at[h, i])
-
-                    if parity == 0:
-                        pl.when(m > 0)(landed)
-                    else:
-                        landed()
-                    for way in range(2):
-                        if exists(way, 1, parity):
-                            pass_on(h, way, 1, i)
-            return carry
-
-        lax.fori_loop(0, size // 2, body, 0)
-
-    def weights_step(d):
-        def body(m, carry):
-            for parity in range(2):
-                i = 2 * m + parity
-                for h in range(2):
-                    for way in range(2):
-                        if exists(way, d, parity):
-                            arrived(h, way, d, i)
-                            if exists(way, d + 1, parity):
-                                pass_on(h, way, d + 1, i)
-            return carry
-
-        lax.fori_loop(0, size // 2, body, 0)
-
-    def spread(src, dst, n):
+        lax.fori_loop(1, hop, body, 0)
+        for h in range(2):
+            for way in range(2):
+                if exists(way, 1, 0):
+                    pass_on(h, way, 1, 0)
+
+    def weights_first(i):
+        for h in range(2):
+            wait(held(h, i, 0), w_first.at[h, i])
+            for way in range(2):
+                if exists(way, 1, i % 2):
+                    pass_on(h, way, 1, i)
+
+    def weights_step(d, i):
+        for h in range(2):
+            for way in range(2):
+                if exists(way, d, i % 2):
+                    wait(held(h, i, (1 - 2 * way) * d), w_ring.at[h, way, d - 1, i])
+                    if exists(way, d + 1, i % 2):
+                        pass_on(h, way, d + 1, i)
+
+    def spread(src, dst, n, first_peer=1, end=nseq):
         def body(i, carry):
             p = (s + i) % nseq
             send(src.at[p], dst.at[s], a2a_send.at[n], a2a_recv.at[n], seq=p)
             return carry
 
-        lax.fori_loop(1, nseq, body, 0)
-        dst[pl.ds(s, 1)] = src[pl.ds(s, 1)]
+        lax.fori_loop(first_peer, end, body, 0)
+        if first_peer == 1:
+            dst[pl.ds(s, 1)] = src[pl.ds(s, 1)]
+
+    def spread_part(src, dst, n, part):
+        piece = nseq // 4
+        spread(src, dst, n, max(1, part * piece), (part + 1) * piece)
 
     def landed(dst, n):
         wait(dst.at[pl.ds(0, nseq - 1)], a2a_recv.at[n])
-
-    loads[0].wait()
-    weights_begin()
-    loads[1].wait()
-    loads[2].wait()
-
-    out16[:, :GROUP, :] = sig[...].astype(F32).T.reshape(nseq, GROUP, LANES).astype(BF16)
-    out16[:, GROUP:, :] = fil[...].astype(F32).T.reshape(nseq, GROUP, LANES).astype(BF16)
-    pl.semaphore_wait(all_in, nz - 1)
-    spread(out16, in16, 0)
-
-    loads[3].wait()
-    send(call.at[c], call.at[c], c_send, c_recv.at[0], chan=sibling)
-    for dx in range(1, nx):
-        send(call.at[c], call.at[c], c_send, c_recv.at[dx], chan=x_peer(dx))
-
-    for load in loads[4:]:
-        load.wait()
-    weights_first()
-    for dx in range(1, nx):
-        ref = call.at[x_peer(-dx)]
-        wait(ref, c_recv.at[dx])
-        send(ref, ref, c_send, c_recv.at[nx - 1 + dx], chan=sibling)
 
     def by_channel(ref, width, start):
         return jnp.concatenate(
@@ -349,51 +373,206 @@
             axis=1,
         )
 
-    weights_step(1)
-
-    landed(in16, 0)
-    rows32[...] = in16[...].astype(F32).reshape(nseq * 2 * GROUP, LANES)
-    sig_x = by_channel(rows32, 2 * GROUP, 0)
-    fil_x = by_channel(rows32, 2 * GROUP, GROUP)
-    sf_spec[0] = forward(sig_x.astype(BF16), first, twist, second)
-    sf_spec[1] = forward(fil_x.astype(BF16), first, twist, second)
-    weights_step(2)
-    conv = inverse(times(sf_spec[0], sf_spec[1]), twist, back, last)
-    to_blocks(rows32, conv + gain(sig_x), GROUP, 0)
-    out8[...] = rows32[pl.ds(0, nseq * GROUP), :].reshape(nseq, GROUP, LANES).astype(BF16)
-    spread(out8, in8, 1)
-
-    for d in range(3, reach + 1):
-        weights_step(d)
-
-    wait(call.at[sibling], c_recv.at[0])
-    for dx in range(1, nx):
-        wait(call.at[((x - dx) % nx) * CORES + (1 - core)], c_recv.at[nx - 1 + dx])
-    total = jnp.zeros((LANES, chans), F32)
-    for n in range(nx * CORES):
-        total += mm(call[n], wt[pl.ds(n * chans, chans), :])
-    grad[...] = total
+
+    def to_all(ref, send_sem, recv_sem):
+        send(ref, ref, send_sem.at[0], recv_sem.at[0], chan=sibling)
+        for dx in range(1, nx):
+            send(ref, ref, send_sem.at[dx], recv_sem.at[dx], chan=x_peer(dx))
+
+    def cotangent_out():
+        ref = ck0.at[1, :, cols0(c)]
+        wait(ref, p_recv.at[0])
+        to_all(ck0.at[:, :, cols0(c)], k0_send, k0_recv)
+
+        @pl.when(keeps)
+        def _():
+            wait(ck1.at[1, :, cols1(x)], p_recv.at[1])
+            to_all(ck1.at[:, :, cols1(x)], k1_send, k1_recv)
+
+    def cotangent_on():
+        for dx in range(1, nx):
+            ref = ck0.at[:, :, cols0(x_peer(-dx))]
+            wait(ref, k0_recv.at[dx])
+            send(ref, ref, k0_send.at[nx - 1 + dx], k0_recv.at[nx - 1 + dx], chan=sibling)
+
+        @pl.when(keeps)
+        def _():
+            for dx in range(1, nx):
+                ref = ck1.at[:, :, cols1((x - dx) % nx)]
+                wait(ref, k1_recv.at[dx])
+                send(ref, ref, k1_send.at[nx - 1 + dx], k1_recv.at[nx - 1 + dx], chan=sibling)
+
+    def cotangent_in():
+        wait(ck0.at[:, :, cols0(sibling)], k0_recv.at[0])
+        for dx in range(1, nx):
+            other = ((x - dx) % nx) * CORES + (1 - core)
+            wait(ck0.at[:, :, cols0(other)], k0_recv.at[nx - 1 + dx])
+
+        @pl.when(jnp.logical_not(keeps))
+        def _():
+            wait(ck1.at[:, :, cols1(x)], k1_recv.at[0])
+            for dx in range(1, nx):
+                wait(ck1.at[:, :, cols1((x - dx) % nx)], k1_recv.at[nx - 1 + dx])
+
+    def tokens_out(part):
+        if part == 0:
+            pl.semaphore_wait(all_in, nz - 1)
+        spread_part(out16, in16, 0, part)
+
+    def transform(n):
+        if n == 0:
+            landed(in16, 0)
+            rows32[...] = in16[...].astype(F32).reshape(nseq * 2 * GROUP, LANES)
+            for load in loads[5:]:
+                load.wait()
+        value = by_channel(rows32, 2 * GROUP, n * GROUP)
+        sf_spec[n] = forward(value.astype(BF16), first, twist, second)
+
+    def convolve():
+        value = inverse(times(sf_spec[0], sf_spec[1]), twist, back, last)
+        value += gain(by_channel(rows32, 2 * GROUP, 0))
+        to_blocks(rows32, value, GROUP, 0)
+        out8[...] = rows32[pl.ds(0, nseq * GROUP), :].reshape(nseq, GROUP, LANES).astype(BF16)
+
+    def before_out(part):
+        spread_part(out8, in8, 1, part)
+
+    def gate():
+        landed(in8, 1)
+        gating[...] = in8[...].astype(F32).reshape(chans, LANES).T
+        gated[0] = (gating[...] * gat[...].astype(F32)).astype(BF16)
+
+    def gate_out():
+        send(gated.at[0], gated.at[1], p_send.at[4], p_recv.at[4], seq=z_pair)
+        send(gated.at[0], gated.at[2], p_send.at[5], p_recv.at[5], seq=y_pair)
+
+    loads[0].wait()
+    loads[1].wait()
+    weights_begin()
+    send(cot_perm.at[:, far], ck0.at[1, :, cols0(c)], p_send.at[0], p_recv.at[0], seq=z_pair)
+
+    @pl.when(jnp.logical_not(keeps))
+    def _():
+        send(
+            cot_perm.at[:, pl.ds(middle, middle)],
+            ck1.at[1, :, cols1(x)],
+            p_send.at[1],
+            p_recv.at[1],
+            seq=y_pair,
+        )
+
+    weights_first(1)
+    tokens_out(0)
+    weights_first(2)
+    tokens_out(1)
+    weights_first(3)
+    tokens_out(2)
+    weights_step(1, 0)
+    tokens_out(3)
+    weights_step(1, 1)
+    cotangent_out()
+    weights_step(1, 2)
+    weights_step(1, 3)
+    weights_step(2, 0)
+    cotangent_on()
+    weights_step(2, 1)
+    weights_step(2, 2)
+    transform(0)
+    weights_step(2, 3)
+    transform(1)
+    weights_step(3, 0)
+    convolve()
+    weights_step(3, 1)
+    before_out(0)
+    weights_step(3, 2)
+    before_out(1)
+    weights_step(3, 3)
+    before_out(2)
+    weights_step(4, 0)
+    before_out(3)
+    cotangent_in()
+    weights_step(4, 1)
+    weights_step(4, 2)
+    weights_step(4, 3)
+    sum0 = mm(ck0[...].reshape(2 * LANES, -1), wt[pl.ds(0, base), :])
+    gp_out[0] = sum0[LANES:].astype(BF16)
+    send(gp_out.at[0], gp_in.at[0], p_send.at[2], p_recv.at[2], seq=z_pair)
+    sum1 = mm(ck1[...].reshape(2 * LANES, -1), wt[pl.ds(base, base), :])
+    gp_out[1] = sum1[LANES:].astype(BF16)
+    send(gp_out.at[1], gp_in.at[1], p_send.at[3], p_recv.at[3], seq=y_pair)
+
+    gate()
+    gate_out()
+    mine = sum0[:LANES] + sum1[:LANES]
+    wait(gp_in.at[0], p_recv.at[2])
+    wait(gp_in.at[1], p_recv.at[3])
     gates = gat[...].astype(F32)
+    total = mine + gp_in[0].astype(F32) + gp_in[1].astype(F32)
     gconv = (total * gates).T
     gout8[...] = gconv.reshape(nseq, GROUP, LANES).astype(BF16)
     spread(gout8, gin8, 2)
-
-    landed(in8, 1)
-    before = in8[...].astype(F32).reshape(chans, LANES).T
-    outs[2] = (grad[...] * before).astype(BF16)
-    gated = (before * gates).astype(BF16)
-
-    def part(n):
-        rows = wt[pl.ds(pl.multiple_of(n * chans, chans), chans), :]
+    outs[2] = (total * gating[...]).astype(BF16)
+
+    wait(gated.at[1], p_recv.at[4])
+    wait(gated.at[2], p_recv.at[5])
+
+    def part(tokens, start, width):
         return lax.dot_general(
-            gated, rows, (((1,), (1,)), ((), ())), preferred_element_type=F32
+            tokens,
+            wt[pl.ds(pl.multiple_of(start, width), width), :],
+            (((1,), (1,)), ((), ())),
+            preferred_element_type=F32,
         )
 
+    z_tokens = jnp.concatenate([gated[0], gated[1]], axis=0)
+    y_tokens = jnp.concatenate([gated[0], gated[2]], axis=0)
+
+    def part0(n):
+        return part(z_tokens, n * quarter, quarter)
+
+    def part1(n):
+        return part(y_tokens, base + n * middle, middle)
+
     for n in range(nx):
-        ex_out[n] = part(n * CORES + (1 - core)).astype(BF16)
-        send(ex_out.at[n], ex_in.at[n], m_send.at[0], m_recv.at[n], chan=sibling)
+        ex0_out[n] = part0(n * CORES + (1 - core)).astype(BF16)
+    send(ex0_out, ex0_in, m0_send.at[0], m0_recv.at[0], chan=sibling)
+
+    @pl.when(jnp.logical_not(keeps))
+    def _():
+        for n in range(nx):
+            ex1_out[n] = part1(n).astype(BF16)
+        send(ex1_out, ex1_in, m1_send.at[0], m1_recv.at[0], chan=sibling)
+
     for n in range(nx):
-        own[n] = part(n * CORES + core)
+        own0[n] = part0(n * CORES + core)
+
+    @pl.when(keeps)
+    def _():
+        for n in range(nx):
+            own1[n] = part1(n)
+        wait(ex1_in, m1_recv.at[0])
+        own1[...] += ex1_in[...].astype(F32)
+        for dx in range(1, nx):
+            mx1_out[dx - 1] = own1[(x + dx) % nx].astype(BF16)
+            send(
+                mx1_out.at[dx - 1],
+                mx1_in.at[dx - 1],
+                m1_send.at[dx],
+                m1_recv.at[dx],
+                chan=x_peer(dx),
+            )
+
+    wait(ex0_in, m0_recv.at[0])
+    own0[...] += ex0_in[...].astype(F32)
+    for dx in range(1, nx):
+        mx0_out[dx - 1] = own0[(x + dx) % nx].astype(BF16)
+        send(
+            mx0_out.at[dx - 1],
+            mx0_in.at[dx - 1],
+            m0_send.at[dx],
+            m0_recv.at[dx],
+            chan=x_peer(dx),
+        )
 
     landed(gin8, 2)
     rows32[pl.ds(0, nseq * GROUP), :] = gin8[...].astype(F32).reshape(nseq * GROUP, LANES)
@@ -406,17 +585,35 @@
     rout16[...] = rows32[...].reshape(nseq, 2 * GROUP, LANES).astype(BF16)
     spread(rout16, rin16, 3)
 
-    for n in range(nx):
-        wait(ex_in.at[n], m_recv.at[n])
-        own[n] += ex_in[n].astype(F32)
+    @pl.when(keeps)
+    def _():
+        result = own1[x]
+        for dx in range(1, nx):
+            wait(mx1_in.at[dx - 1], m1_recv.at[dx])
+            result += mx1_in[dx - 1].astype(F32)
+        perm[:, middle:] = result[:LANES].astype(BF16)
+        ret1_out[...] = result[LANES:].astype(BF16)
+        send(ret1_out, ret1_in, p_send.at[7], p_recv.at[7], seq=y_pair)
+
+    result = own0[x]
     for dx in range(1, nx):
-        mx_out[dx - 1] = own[(x + dx) % nx].astype(BF16)
-        send(mx_out.at[dx - 1], mx_in.at[dx - 1], m_send.at[1], m_recv.at[nx + dx], chan=x_peer(dx))
-    result = own[x]
-    for dx in range(1, nx):
-        wait(mx_in.at[dx - 1], m_recv.at[nx + dx])
-        result += mx_in[dx - 1].astype(F32)
-    outs[0] = result.astype(BF16)
+        wait(mx0_in.at[dx - 1], m0_recv.at[dx])
+        result += mx0_in[dx - 1].astype(F32)
+    perm[:, near] = result[:LANES].astype(BF16)
+    ret0_out[...] = result[LANES:].astype(BF16)
+    send(ret0_out, ret0_in, p_send.at[6], p_recv.at[6], seq=z_pair)
+
+    wait(ret0_in, p_recv.at[6])
+    perm[:, far] = ret0_in[...]
+
+    @pl.when(jnp.logical_not(keeps))
+    def _():
+        wait(ret1_in, p_recv.at[7])
+        perm[:, middle:] = ret1_in[...]
+
+    outs[0] = lax.dot_general(
+        perm[...], order[...], (((1,), (1,)), ((), ())), preferred_element_type=F32
+    ).astype(BF16)
 
     landed(rin16, 3)
     grads = rin16[...].astype(F32)
@@ -425,16 +622,39 @@
 
     for n, src in enumerate((out16, out8, gout8, rout16)):
         wait(src.at[pl.ds(0, nseq - 1)], a2a_send.at[n])
-    wait(wt.at[pl.ds(0, (nseq - 1) * block)], w_send)
-    wait(call.at[pl.ds(0, 2 * nx - 1)], c_send)
-    wait(ex_out, m_send.at[0])
-    wait(mx_out, m_send.at[1])
+    wait(wt.at[pl.ds(0, (2 * (hop - 1) + 2 * hop * (2 * reach - 1)) * half)], w_send)
+    for n in range(2 * nx - 1):
+        wait(ck0.at[:, :, cols0(0)], k0_send.at[n])
+    wait(ck0.at[1, :, cols0(0)], p_send.at[0])
+    wait(gp_out.at[0], p_send.at[2])
+    wait(gp_out.at[1], p_send.at[3])
+    wait(gated.at[0], p_send.at[4])
+    wait(gated.at[0], p_send.at[5])
+    wait(ret0_out, p_send.at[6])
+    wait(ex0_out, m0_send.at[0])
+    for dx in range(1, nx):
+        wait(mx0_out.at[dx - 1], m0_send.at[dx])
+
+    @pl.when(keeps)
+    def _():
+        for n in range(2 * nx - 1):
+            wait(ck1.at[:, :, cols1(0)], k1_send.at[n])
+        for dx in range(1, nx):
+            wait(mx1_out.at[dx - 1], m1_send.at[dx])
+        wait(ret1_out, p_send.at[7])
+
+    @pl.when(jnp.logical_not(keeps))
+    def _():
+        wait(ck1.at[1, :, cols1(0)], p_send.at[1])
+        wait(ex1_out, m1_send.at[0])
 
 
 def local(ny, nz, nx, signal, gates, filters, skip_gain, out_proj, cotangent):
     nseq = ny * nz
     chans = signal.shape[1]
-    block = out_proj.shape[1]
+    half = out_proj.shape[1] // 2
+    quarter, middle = chans // 4, chans // 2
+    hop = ny // 2
     first, twist, second, back, last = make_tables(nseq)
     rows = twist.shape[1]
     hbm = pl.BlockSpec(memory_space=pltpu.HBM)
@@ -458,7 +678,7 @@
             pltpu.VMEM(second.shape, BF16),
             pltpu.VMEM(back.shape, BF16),
             pltpu.VMEM(last.shape, BF16),
-            pltpu.SemaphoreType.DMA((10,)),
+            pltpu.SemaphoreType.DMA((11,)),
             pltpu.VMEM(wide, BF16),
             pltpu.VMEM(wide, BF16),
             pltpu.VMEM(narrow, BF16),
@@ -469,23 +689,46 @@
             pltpu.VMEM(wide, BF16),
             pltpu.VMEM((nseq * 2 * GROUP, LANES), F32),
             pltpu.VMEM((2, GROUP * rows, 2 * LANES), F32),
-            pltpu.VMEM((nseq * block, chans), BF16),
-            pltpu.VMEM((nx * CORES,) + tile, BF16),
+            pltpu.VMEM((nseq * half, chans), BF16),
+            pltpu.VMEM((chans, chans), BF16),
+            pltpu.VMEM(tile, BF16),
+            pltpu.VMEM(tile, BF16),
+            pltpu.VMEM((2, LANES, nx * CORES * quarter), BF16),
+            pltpu.VMEM((2, LANES, nx * middle), BF16),
+            pltpu.VMEM((2,) + tile, BF16),
+            pltpu.VMEM((2,) + tile, BF16),
+            pltpu.VMEM((3,) + tile, BF16),
+            pltpu.VMEM((nx, 2 * LANES, quarter), F32),
+            pltpu.VMEM((nx, 2 * LANES, middle), F32),
+            pltpu.VMEM((nx, 2 * LANES, quarter), BF16),
+            pltpu.VMEM((nx, 2 * LANES, quarter), BF16),
+            pltpu.VMEM((nx, 2 * LANES, middle), BF16),
+            pltpu.VMEM((nx, 2 * LANES, middle), BF16),
+            pltpu.VMEM((nx - 1, 2 * LANES, quarter), BF16),
+            pltpu.VMEM((nx - 1, 2 * LANES, quarter), BF16),
+            pltpu.VMEM((nx - 1, 2 * LANES, middle), BF16),
+            pltpu.VMEM((nx - 1, 2 * LANES, middle), BF16),
+            pltpu.VMEM((LANES, quarter), BF16),
+            pltpu.VMEM((LANES, quarter), BF16),
+            pltpu.VMEM((LANES, middle), BF16),
+            pltpu.VMEM((LANES, middle), BF16),
+            pltpu.VMEM(tile, BF16),
             pltpu.VMEM(tile, F32),
-            pltpu.VMEM((nx,) + tile, F32),
-            pltpu.VMEM((nx,) + tile, BF16),
-            pltpu.VMEM((nx,) + tile, BF16),
-            pltpu.VMEM((nx - 1,) + tile, BF16),
-            pltpu.VMEM((nx - 1,) + tile, BF16),
             pltpu.SemaphoreType.DMA((4,)),
             pltpu.SemaphoreType.DMA((4,)),
             pltpu.SemaphoreType.DMA,
-            pltpu.SemaphoreType.DMA((2, ny)),
-            pltpu.SemaphoreType.DMA((2, 2, ny // 2, ny)),
-            pltpu.SemaphoreType.DMA,
+            pltpu.SemaphoreType.DMA((2, hop)),
+            pltpu.SemaphoreType.DMA((2, 2, ny // 2, hop)),
             pltpu.SemaphoreType.DMA((2 * nx,)),
-            pltpu.SemaphoreType.DMA((2,)),
             pltpu.SemaphoreType.DMA((2 * nx,)),
+            pltpu.SemaphoreType.DMA((2 * nx,)),
+            pltpu.SemaphoreType.DMA((2 * nx,)),
+            pltpu.SemaphoreType.DMA((8,)),
+            pltpu.SemaphoreType.DMA((8,)),
+            pltpu.SemaphoreType.DMA((nx,)),
+            pltpu.SemaphoreType.DMA((nx,)),
+            pltpu.SemaphoreType.DMA((nx,)),
+            pltpu.SemaphoreType.DMA((nx,)),
             pltpu.SemaphoreType.REGULAR,
         ],
         compiler_params=pltpu.CompilerParams(

time: 76.6 us -> 70.9 us (0.926)
  Pallas kernels: 73.4 us -> 68.2 us
    pallas_call x1, Pallas kernels: 73.4 us -> 68.2 us  [local(): pl.pallas_call(functools.partial(kernel, ny, nz, nx), out_shape=jax.Shape...]
where the time goes in v3:
time: 70.9 us; the launch traced here: 70.7 us
  Pallas kernels  68.2 us (96%)
  local copies, waits for them, and re-layouts  1.89 us (3%)
    pallas_call x1, Pallas kernels, local(): pl.pallas_call(functools.partial(kernel, ny, nz, nx), out_shape=jax.Shape...  68.2 us
    squeeze x1, local copies, waits for them, and re-layouts, local(): return tuple((results[n] for n in range(4)))  1.89 us

profile of v3, /device:TPU:6, one launch (start us, length us, event | category | flops | bytes accessed | tf_op | source)
XLA Modules:
  0.0 70.7 jit_solution(2957523447690860564)
XLA Ops:
  0.6 68.2 %shard_map.138 = bf16[4,128,512]{2,1,0:T(8,128)(2,1)} custom-call(f32[512]{0:T(512)} %skip.1, bf16[128,512]{1,0:T(8,128)(2,1)} %sig_hbm.1, bf16[128,512]{1,0:T(8,128)(2,1)} %gat_hbm.1, bf16[128,512]{1,0:T(8,128)(2,1)} %fil_hbm.1, bf16[64,512]{1,0:T(8,128)(2,1)} %bitcast.9, bf16[128,512]{1,0:T(8,128)(2,1)} %cot_hbm.1, ...), custom_call_target="tpu_custom_call" | custom-call | tf_op jit(solution)/shard_map/pallas_call | solution.py:667
  68.8 1.9 %slice_bitcast_fusion = (bf16[128,512]{1,0:T(8,128)(2,1)}, bf16[128,512]{1,0:T(8,128)(2,1)}, bf16[128,512]{1,0:T(8,128)(2,1)}, bf16[128,512]{1,0:T(8,128)(2,1)}) fusion(bf16[4,128,512]{2,1,0:T(8,128)(2,1)} %shard_map.138), kind=kLoop, calls=%fused_computation | loop fusion | bytes 1048576 | tf_op jit(solution)/shard_map/squeeze | solution.py:750

commit v4 on v3

--- a/solution.py
+++ b/solution.py
@@ -338,19 +338,21 @@
                     if exists(way, d + 1, i % 2):
                         pass_on(h, way, d + 1, i)
 
-    def spread(src, dst, n, first_peer=1, end=nseq):
-        def body(i, carry):
-            p = (s + i) % nseq
+    def hops(step, size):
+        return min(step, size - step)
+
+    steps = sorted(
+        ((dy, dz) for dy in range(ny) for dz in range(nz) if dy or dz),
+        key=lambda step: -hops(step[0], ny) - hops(step[1], nz),
+    )
+
+    def spread(src, dst, n, part=0, parts=1):
+        piece = nseq // parts
+        for dy, dz in steps[part * piece : (part + 1) * piece]:
+            p = ((y + dy) % ny) * nz + (z + dz) % nz
             send(src.at[p], dst.at[s], a2a_send.at[n], a2a_recv.at[n], seq=p)
-            return carry
-
-        lax.fori_loop(first_peer, end, body, 0)
-        if first_peer == 1:
+        if part == 0:
             dst[pl.ds(s, 1)] = src[pl.ds(s, 1)]
-
-    def spread_part(src, dst, n, part):
-        piece = nseq // 4
-        spread(src, dst, n, max(1, part * piece), (part + 1) * piece)
 
     def landed(dst, n):
         wait(dst.at[pl.ds(0, nseq - 1)], a2a_recv.at[n])
@@ -417,7 +419,7 @@
     def tokens_out(part):
         if part == 0:
             pl.semaphore_wait(all_in, nz - 1)
-        spread_part(out16, in16, 0, part)
+        spread(out16, in16, 0, part, 4)
 
     def transform(n):
         if n == 0:
@@ -435,7 +437,7 @@
         out8[...] = rows32[pl.ds(0, nseq * GROUP), :].reshape(nseq, GROUP, LANES).astype(BF16)
 
     def before_out(part):
-        spread_part(out8, in8, 1, part)
+        spread(out8, in8, 1, part, 4)
 
     def gate():
         landed(in8, 1)
@@ -462,48 +464,47 @@
         )
 
     weights_first(1)
+    weights_first(3)
+    weights_first(2)
+    cotangent_out()
+    weights_step(1, 0)
     tokens_out(0)
-    weights_first(2)
+    weights_step(1, 1)
     tokens_out(1)
-    weights_first(3)
+    weights_step(1, 3)
     tokens_out(2)
-    weights_step(1, 0)
+    weights_step(1, 2)
     tokens_out(3)
-    weights_step(1, 1)
-    cotangent_out()
-    weights_step(1, 2)
-    weights_step(1, 3)
     weights_step(2, 0)
     cotangent_on()
     weights_step(2, 1)
+    weights_step(2, 3)
     weights_step(2, 2)
     transform(0)
-    weights_step(2, 3)
+    weights_step(3, 0)
     transform(1)
-    weights_step(3, 0)
+    weights_step(3, 1)
     convolve()
-    weights_step(3, 1)
+    weights_step(3, 3)
     before_out(0)
     weights_step(3, 2)
     before_out(1)
-    weights_step(3, 3)
+    weights_step(4, 0)
     before_out(2)
-    weights_step(4, 0)
+    weights_step(4, 1)
     before_out(3)
     cotangent_in()
-    weights_step(4, 1)
+    weights_step(4, 3)
     weights_step(4, 2)
-    weights_step(4, 3)
-    sum0 = mm(ck0[...].reshape(2 * LANES, -1), wt[pl.ds(0, base), :])
-    gp_out[0] = sum0[LANES:].astype(BF16)
+
+    gp_out[0] = mm(ck0[1], wt[pl.ds(0, base), :]).astype(BF16)
     send(gp_out.at[0], gp_in.at[0], p_send.at[2], p_recv.at[2], seq=z_pair)
-    sum1 = mm(ck1[...].reshape(2 * LANES, -1), wt[pl.ds(base, base), :])
-    gp_out[1] = sum1[LANES:].astype(BF16)
+    gp_out[1] = mm(ck1[1], wt[pl.ds(base, base), :]).astype(BF16)
     send(gp_out.at[1], gp_in.at[1], p_send.at[3], p_recv.at[3], seq=y_pair)
+    mine = mm(ck0[0], wt[pl.ds(0, base), :]) + mm(ck1[0], wt[pl.ds(base, base), :])
 
     gate()
     gate_out()
-    mine = sum0[:LANES] + sum1[:LANES]
     wait(gp_in.at[0], p_recv.at[2])
     wait(gp_in.at[1], p_recv.at[3])
     gates = gat[...].astype(F32)

time: 70.9 us -> 68.4 us (0.965)
  Pallas kernels: 68.2 us -> 65.5 us
    pallas_call x1, Pallas kernels: 68.2 us -> 65.5 us  [local(): pl.pallas_call(functools.partial(kernel, ny, nz, nx), out_shape=jax.Shape...]
where the time goes in v4:
time: 68.4 us; the launch traced here: 68 us
  Pallas kernels  65.5 us (96%)
  local copies, waits for them, and re-layouts  1.89 us (3%)
    pallas_call x1, Pallas kernels, local(): pl.pallas_call(functools.partial(kernel, ny, nz, nx), out_shape=jax.Shape...  65.5 us
    squeeze x1, local copies, waits for them, and re-layouts, local(): return tuple((results[n] for n in range(4)))  1.89 us

profile of v4, /device:TPU:6, one launch (start us, length us, event | category | flops | bytes accessed | tf_op | source)
XLA Modules:
  0.0 68.0 jit_solution(5356282184371604743)
XLA Ops:
  0.6 65.5 %shard_map.138 = bf16[4,128,512]{2,1,0:T(8,128)(2,1)} custom-call(f32[512]{0:T(512)} %skip.1, bf16[128,512]{1,0:T(8,128)(2,1)} %sig_hbm.1, bf16[128,512]{1,0:T(8,128)(2,1)} %gat_hbm.1, bf16[128,512]{1,0:T(8,128)(2,1)} %fil_hbm.1, bf16[64,512]{1,0:T(8,128)(2,1)} %bitcast.9, bf16[128,512]{1,0:T(8,128)(2,1)} %cot_hbm.1, ...), custom_call_target="tpu_custom_call" | custom-call | tf_op jit(solution)/shard_map/pallas_call | solution.py:668
  66.1 1.9 %slice_bitcast_fusion = (bf16[128,512]{1,0:T(8,128)(2,1)}, bf16[128,512]{1,0:T(8,128)(2,1)}, bf16[128,512]{1,0:T(8,128)(2,1)}, bf16[128,512]{1,0:T(8,128)(2,1)}) fusion(bf16[4,128,512]{2,1,0:T(8,128)(2,1)} %shard_map.138), kind=kLoop, calls=%fused_computation | loop fusion | bytes 1048576 | tf_op jit(solution)/shard_map/squeeze | solution.py:751

commit v5 on v4

--- a/solution.py
+++ b/solution.py
@@ -77,7 +77,7 @@
     mid = mm(high, back[0]) + mm(low, back[0]) + mm(high, back[1])
     cos, sin = twist[0], twist[1]
     pieces = []
-    for c in range(GROUP):
+    for c in range(spec.shape[0] // rows):
         re = mid[c * rows : (c + 1) * rows, :LANES]
         im = mid[c * rows : (c + 1) * rows, LANES:]
         pieces.append(jnp.concatenate([re * cos + im * sin, im * cos - re * sin], axis=0))
@@ -579,8 +579,9 @@
     rows32[pl.ds(0, nseq * GROUP), :] = gin8[...].astype(F32).reshape(nseq * GROUP, LANES)
     grad_x = by_channel(rows32, GROUP, 0)
     g_spec = forward(grad_x.astype(BF16), first, twist, second)
-    through = inverse(times_conj(sf_spec[1], g_spec), twist, back, last)
-    kern = inverse(times_conj(sf_spec[0], g_spec), twist, back, last)
+    products = [times_conj(sf_spec[1], g_spec), times_conj(sf_spec[0], g_spec)]
+    both = inverse(jnp.concatenate(products, axis=0), twist, back, last)
+    through, kern = both[:, : GROUP * LANES], both[:, GROUP * LANES :]
     to_blocks(rows32, through + gain(grad_x), 2 * GROUP, 0)
     to_blocks(rows32, kern * (1.0 / math.sqrt(nseq * LANES)), 2 * GROUP, GROUP)
     rout16[...] = rows32[...].reshape(nseq, 2 * GROUP, LANES).astype(BF16)

time: 68.4 us -> 68.3 us (level)
  no operation moved by 1% of the time
where the time goes in v5:
time: 68.3 us; the launch traced here: 68 us
  Pallas kernels  65.5 us (96%)
  local copies, waits for them, and re-layouts  1.89 us (3%)
    pallas_call x1, Pallas kernels, local(): pl.pallas_call(functools.partial(kernel, ny, nz, nx), out_shape=jax.Shape...  65.5 us
    squeeze x1, local copies, waits for them, and re-layouts, local(): return tuple((results[n] for n in range(4)))  1.89 us

profile of v5, /device:TPU:6, one launch (start us, length us, event | category | flops | bytes accessed | tf_op | source)
XLA Modules:
  0.0 68.0 jit_solution(10278273929335354268)
XLA Ops:
  0.6 65.5 %shard_map.138 = bf16[4,128,512]{2,1,0:T(8,128)(2,1)} custom-call(f32[512]{0:T(512)} %skip.1, bf16[128,512]{1,0:T(8,128)(2,1)} %sig_hbm.1, bf16[128,512]{1,0:T(8,128)(2,1)} %gat_hbm.1, bf16[128,512]{1,0:T(8,128)(2,1)} %fil_hbm.1, bf16[64,512]{1,0:T(8,128)(2,1)} %bitcast.9, bf16[128,512]{1,0:T(8,128)(2,1)} %cot_hbm.1, ...), custom_call_target="tpu_custom_call" | custom-call | tf_op jit(solution)/shard_map/pallas_call | solution.py:669
  66.1 1.9 %slice_bitcast_fusion = (bf16[128,512]{1,0:T(8,128)(2,1)}, bf16[128,512]{1,0:T(8,128)(2,1)}, bf16[128,512]{1,0:T(8,128)(2,1)}, bf16[128,512]{1,0:T(8,128)(2,1)}) fusion(bf16[4,128,512]{2,1,0:T(8,128)(2,1)} %shard_map.138), kind=kLoop, calls=%fused_computation | loop fusion | bytes 1048576 | tf_op jit(solution)/shard_map/squeeze | solution.py:752
